TPU v7x, 256 devices: a whole 4x4x8 slice. The times are simulated.
256 devices in a mesh: pipe: 8 (over z), tensor: 4 (over x_hi, core), dp: 8 (over x_lo, y).
Axes of the slice: x: 4 (x_hi: 2, x_lo: 2; x = x_hi * 2 + x_lo), y: 4, z: 8, core: 2. Of those that a mesh axis runs over, the one named last changes fastest.
Arguments:
- norm_input: bfloat16 [8, 4, 512, 8192], P('pipe', None, 'dp', 'tensor'), may hold values from -256 to 256
- gain: float32 [8, 8192], P('pipe', 'tensor'), may hold values from 0.25 to 1.75
- value_weight: bfloat16 [8, 8192, 1024], P('pipe', 'tensor'), may hold values from -0.0625 to 0.0625
- shrink_factor_matrices: bfloat16 [8, 8, 8192, 64], P('pipe', None, 'tensor'), may hold values from -0.0625 to 0.0625
- expand_factor_matrices: bfloat16 [8, 8, 64, 1024], P('pipe'), may hold values from -0.1875 to 0.1875
- value_gradient: bfloat16 [8, 4, 512, 1024], P('pipe', None, 'dp'), may hold values from -6 to 6
- candidate_index: int32 [4, 32], P(None, 'dp'), may hold values from 0 to 7
- counts: int32 [8], replicated, may hold values from 128 to 512
Outputs:
- grad_in: bfloat16 [8, 4, 512, 8192], P('pipe', None, 'dp', 'tensor')
- grad_down: float32 [8, 8, 8192, 64], P('pipe', 'dp', 'tensor')
- grad_up: float32 [8, 8, 64, 1024], P('pipe', 'dp', None, 'tensor')
All inputs are finite; a program needn't handle non-finite values.
Results may differ from a plain program's by a relative error of at most 0.0055.
Values sent between devices are 32-bit elements; how exact they have to be, the bound alone decides.
No kernel may reach another device: no remote copies, remote signals or barrier semaphores. Data moves between devices by JAX's collectives and lax.ppermute only.
A program may use at most 128 MiB of HBM per device.

v0:
```python
import functools

import jax
import jax.numpy as jnp
from jax import lax
from jax.experimental import pallas as pl
from jax.experimental.pallas import tpu as pltpu
from jax.sharding import PartitionSpec as P

MODEL_WIDTH = 8192
BLOCK_ROWS = 16
RANK = 64
ADAPTER_SCALE = 2.0
EPS = 1e-06
FIRST_BLOCK = 512
PART_COLUMNS = (256, 1024)
SWAP_COLUMNS = 384
VMEM_LIMIT = 16 * 1024 * 1024
FIRST_VMEM_LIMIT = 64 * 1024 * 1024
NT = (((1,), (1,)), ((), ()))
NN = (((1,), (0,)), ((), ()))
F32 = jnp.float32
BF16 = jnp.bfloat16


def dot(a, b, dims):
    return lax.dot_general(a, b, dims, preferred_element_type=F32)


def first_kernel(
    total_tokens,
    cand_hbm,
    counts_hbm,
    h_hbm,
    gain_hbm,
    weight_hbm,
    shrink_hbm,
    expand_hbm,
    grad_hbm,
    gained_dn_out,
    normed_out,
    scaled_part_out,
    back_out,
    mask_out,
    stat_out,
    gained_dn_ref,
    normed_ref,
    scaled_part_ref,
    back_ref,
    mask_ref,
    stat_ref,
    cand_ref,
    counts_ref,
    h_ref,
    gain_ref,
    weight_ref,
    shrink_ref,
    expand_ref,
    grad_ref,
    scaled_ref,
    sel_ref,
    low_ref,
    sems,
    out_sems,
):
    n_rows, features = h_ref.shape
    n_sel = back_ref.shape[1]
    n_blocks = n_rows // BLOCK_ROWS
    per_micro = cand_ref.shape[1]
    n_cand = counts_ref.shape[0]
    kv_local = scaled_part_ref.shape[1]
    fb = FIRST_BLOCK
    n_steps = features // fb
    pairs = [
        (cand_hbm, cand_ref),
        (counts_hbm, counts_ref),
        (grad_hbm, grad_ref),
        (expand_hbm, expand_ref),
        (h_hbm, h_ref),
        (gain_hbm, gain_ref),
        (shrink_hbm, shrink_ref),
    ]
    copies = [
        pltpu.make_async_copy(source, target, sems.at[i]) for i, (source, target) in enumerate(pairs)
    ]
    for step in range(n_steps):
        rows = pl.ds(step * fb, fb)
        copies.append(
            pltpu.make_async_copy(
                weight_hbm.at[rows, :], weight_ref.at[rows, :], sems.at[len(pairs) + step]
            )
        )
    for copy in copies:
        copy.start()
    for copy in copies[:3]:
        copy.wait()

    leaving = []

    def leave(source, target):
        copy = pltpu.make_async_copy(source, target, out_sems.at[len(leaving)])
        copy.start()
        leaving.append(copy)

    owner = lax.broadcasted_iota(jnp.int32, (BLOCK_ROWS, n_sel), 1) // RANK
    for block in range(n_blocks):
        cand = cand_ref[block // per_micro, block % per_micro]
        count = jnp.full((BLOCK_ROWS, 1), counts_ref[cand], jnp.int32).astype(F32)
        weight = total_tokens / (n_cand * count)
        rows = pl.ds(block * BLOCK_ROWS, BLOCK_ROWS)
        scaled_ref[rows, :] = (grad_ref[rows, :].astype(F32) * weight).astype(BF16)
        mask_ref[rows, :] = jnp.where(owner == cand, 1.0, 0.0).astype(BF16)
    first_column = pl.multiple_of(lax.axis_index("tensor") * kv_local, kv_local)
    scaled_part_ref[...] = scaled_ref[:, pl.ds(first_column, kv_local)]
    leave(scaled_part_ref, scaled_part_out)
    leave(mask_ref, mask_out)
    copies[3].wait()
    back = dot(scaled_ref[...], expand_ref[...], NT) * mask_ref[...].astype(F32)
    back_ref[...] = back
    leave(back_ref, back_out)
    sel_ref[...] = back.astype(BF16)
    copies[4].wait()
    copies[5].wait()
    copies[6].wait()

    sumsq = jnp.zeros((n_rows, 1), F32)
    proj = jnp.zeros((n_rows, 1), F32)
    for step in range(n_steps):
        columns = pl.ds(step * fb, fb)
        h16 = h_ref[:, columns]
        h = h16.astype(F32)
        gain = gain_ref[:, columns]
        gained = h * gain
        normed = gained.astype(BF16)
        normed_ref[:, columns] = normed
        leave(normed_ref.at[:, columns], normed_out.at[:, columns])
        shrink = shrink_ref[:, columns]
        low = dot(normed, shrink, NT)
        if step == 0:
            low_ref[...] = low
        else:
            low_ref[...] += low
        sumsq += jnp.sum(h * h, axis=1, keepdims=True)
        adapter = dot(sel_ref[...], shrink, NN)
        copies[len(pairs) + step].wait()
        dn = dot(scaled_ref[...], weight_ref[columns, :], NT) + ADAPTER_SCALE * adapter
        gained_dn_ref[:, columns] = gain * dn
        leave(gained_dn_ref.at[:, columns], gained_dn_out.at[:, columns])
        proj += jnp.sum(gained * dn, axis=1, keepdims=True)

    masked = low_ref[...] * mask_ref[...].astype(F32)
    folded = masked[:, : 2 * RANK]
    for part in range(1, n_sel // (2 * RANK)):
        folded += masked[:, part * 2 * RANK : (part + 1) * 2 * RANK]
    folded += pltpu.roll(folded, RANK, 1)
    lane = lax.broadcasted_iota(jnp.int32, (n_rows, 2 * RANK), 1)
    stat_ref[...] = jnp.where(
        lane < RANK,
        folded,
        jnp.where(lane == RANK, sumsq, jnp.where(lane == RANK + 1, proj, 0.0)),
    )
    leave(stat_ref, stat_out)
    for copy in leaving:
        copy.wait()


def quarters():
    odd = lax.rem(lax.axis_index("pipe"), 2)
    return odd, (1 + 2 * odd, 2 - 2 * odd, odd, 3 - odd)


def rows_of(quarter, size):
    return pl.ds(pl.multiple_of(quarter * size, size), size)


def contrib_kernel(
    here_ref,
    there_ref,
    gained_dn_ref,
    h_hbm,
    up_ref,
    down_ref,
    first_ref,
    second_ref,
    h_ref,
    sems,
):
    size = up_ref.shape[0]
    order = quarters()[1]
    loads = []
    for i, quarter in enumerate(order):
        rows = rows_of(quarter, size)
        loads.append(pltpu.make_async_copy(h_hbm.at[rows, :], h_ref.at[rows, :], sems.at[i]))
    for copy in loads:
        copy.start()
    for i, target in enumerate((up_ref, down_ref, first_ref, second_ref)):
        rows = rows_of(order[i], size)
        stat = here_ref[rows, :] + there_ref[rows, :]
        rms = jnp.sqrt(stat[:, RANK : RANK + 1] / MODEL_WIDTH + EPS)
        inv = 1.0 / rms
        proj = stat[:, RANK + 1 : RANK + 2] / (MODEL_WIDTH * rms * rms * rms)
        loads[i].wait()
        target[...] = gained_dn_ref[rows, :] * inv - h_ref[rows, :].astype(F32) * proj


def pair_kernel(first_ref, second_ref, from_below_ref, from_above_ref, pair_ref):
    section = lax.axis_index("pipe")
    last = lax.axis_size("pipe") - 1
    odd = lax.rem(section, 2)
    owners, rows2, _ = pair_ref.shape
    rows = rows2 // 2
    for owner in range(owners):
        part = pl.ds(owner * rows, rows)
        below = from_below_ref[part, :]
        above = from_above_ref[part, :]
        pair_ref[owner, :rows, :] = first_ref[part, :] + jnp.where(odd == 1, below, above)
        mine = jnp.where(section == 0, 0.0, second_ref[part, :])
        other = jnp.where(odd == 1, above, below)
        pair_ref[owner, rows:, :] = mine + jnp.where(section == last, 0.0, other)


def scan_kernel(owned_ref, after_ref):
    groups, rows2, _ = owned_ref.shape
    rows = rows2 // 2
    total = jnp.zeros((rows, owned_ref.shape[2]), F32)
    for group in range(groups - 1, -1, -1):
        after_ref[group, :rows, :] = total
        if group:
            total = total + owned_ref[group, :rows, :]
    shift = 1 - lax.rem(lax.axis_index("pipe"), 2)
    places = [lax.rem(group + shift, groups) for group in range(groups)]
    total = owned_ref[places[groups - 1], rows:, :]
    for group in range(groups - 2, -1, -1):
        after_ref[places[group], rows:, :] = total
        total = total + owned_ref[places[group], rows:, :]
    after_ref[places[groups - 1], rows:, :] = total


def spread_kernel(after_ref, first_ref, second_ref, up_ref, down_ref):
    section = lax.axis_index("pipe")
    odd = lax.rem(section, 2)
    owners, rows2, _ = after_ref.shape
    rows = rows2 // 2
    for owner in range(owners):
        part = pl.ds(owner * rows, rows)
        after_first = after_ref[owner, :rows, :]
        after_second = after_ref[owner, rows:, :]
        up_ref[part, :] = jnp.where(odd == 1, after_second, after_first)
        down = jnp.where(
            odd == 1, after_first + first_ref[part, :], after_second + second_ref[part, :]
        )
        down_ref[part, :] = jnp.where(section == 0, 0.0, down)


def final_kernel(
    after_ref,
    up_ref,
    down_ref,
    first_ref,
    second_ref,
    from_below_ref,
    from_above_ref,
    last_below_ref,
    last_above_ref,
    out_ref,
):
    section = lax.axis_index("pipe")
    last = lax.axis_size("pipe") - 1
    odd, (up, down, first, second) = quarters()
    owners, rows2, _ = after_ref.shape
    rows = rows2 // 2
    size = owners * rows
    for owner in range(owners):
        part = pl.ds(owner * rows, rows)

        def place(quarter):
            return pl.ds(pl.multiple_of(quarter * size + owner * rows, rows), rows)

        above = from_above_ref[part, :]
        after = after_ref[owner, :rows, :] + jnp.where(odd == 1, 0.0, above)
        out_ref[place(first), :] = (after + first_ref[part, :]).astype(BF16)
        after = after_ref[owner, rows:, :] + jnp.where(odd == 1, above, 0.0)
        after = jnp.where(section == last, 0.0, after)
        out_ref[place(second), :] = (after + second_ref[part, :]).astype(BF16)
        out_ref[place(up), :] = (last_above_ref[part, :] + up_ref[part, :]).astype(BF16)
        out_ref[place(down), :] = (last_below_ref[part, :] + down_ref[part, :]).astype(BF16)


def adapter_kernel(
    here_ref,
    there_ref,
    back_ref,
    mask_ref,
    normed_ref,
    scaled_ref,
    *refs,
):
    *parts, norm_sel_ref, low_sel_ref = refs
    n_parts = len(PART_COLUMNS) + 1
    swaps = parts[2 * n_parts :]
    ring = len(swaps)
    n_rows, n_sel = back_ref.shape
    features = normed_ref.shape[1]
    half = n_sel // 2
    stat = here_ref[...] + there_ref[...]
    rms = jnp.sqrt(stat[:, RANK : RANK + 1] / MODEL_WIDTH + EPS)
    norm_sel_ref[...] = (back_ref[...] / rms).T.astype(BF16)
    lane = lax.broadcasted_iota(jnp.int32, (n_rows, 2 * RANK), 1)
    low = jnp.where(lane < RANK, stat / rms, 0.0)
    low = low + pltpu.roll(low, RANK, 1)
    low = jnp.concatenate([low] * (n_sel // (2 * RANK)), axis=1)
    low_sel_ref[...] = (low * mask_ref[...].astype(F32)).T.astype(BF16)
    mine = lax.axis_index("dp") // ring
    for targets, part in ((parts[n_parts : 2 * n_parts], 1 - mine), (parts[:n_parts], mine)):
        rows = rows_of(part, half)
        norm_sel = norm_sel_ref[rows, :]
        start = 0
        for i, target in enumerate(targets):
            if i == n_parts - 1:
                start += SWAP_COLUMNS
            width = min(target.shape[1], features - start)
            for offset in range(0, width, FIRST_BLOCK):
                size = min(FIRST_BLOCK, width - offset)
                normed = normed_ref[:, start + offset : start + offset + size]
                target[:, offset : offset + size] = ADAPTER_SCALE * dot(norm_sel, normed, NN)
            start += width
            if width < target.shape[1]:
                target[:, width:] = ADAPTER_SCALE * dot(low_sel_ref[rows, :], scaled_ref[...], NN)
    start = sum(PART_COLUMNS)
    normed = normed_ref[:, start : start + SWAP_COLUMNS]
    mine = lax.rem(lax.axis_index("dp"), ring)
    for shift, target in enumerate(swaps):
        owner = lax.rem(mine + shift, ring)
        for upper in range(2):
            norm_sel = norm_sel_ref[rows_of(upper * ring + owner, RANK), :]
            target[upper * RANK : (upper + 1) * RANK, :] = ADAPTER_SCALE * dot(norm_sel, normed, NN)


def split_kernel(keep_ref, come_ref, own_ref, *send_refs):
    parts = keep_ref.shape[0] // RANK
    mine = lax.rem(lax.axis_index("dp"), parts)
    for shift, target in enumerate((own_ref, *send_refs)):
        rows = rows_of(lax.rem(mine + shift, parts), RANK)
        target[...] = keep_ref[rows, :] + come_ref[rows, :]


def sum_kernel(*refs):
    total = refs[0][...]
    for ref in refs[1:-1]:
        total = total + ref[...]
    refs[-1][...] = total


def swap_kernel(*refs):
    *shares, keep_ref, send_ref, total_ref = refs
    total = shares[0][...]
    for ref in shares[1:]:
        total = total + ref[...]
    total_ref[...] = total
    mine = lax.axis_index("dp") // len(shares)
    keep_ref[...] = total_ref[rows_of(mine, RANK), :]
    send_ref[...] = total_ref[rows_of(1 - mine, RANK), :]


def gather_kernel(part_0_ref, part_1_ref, swap_keep_ref, swap_come_ref, *refs):
    *shares, down_ref, up_ref = refs
    total = shares[0][...]
    for ref in shares[1:]:
        total = total + ref[...]
    start = 0
    for value in (part_0_ref[...], part_1_ref[...], swap_keep_ref[...] + swap_come_ref[...]):
        down_ref[:, start : start + value.shape[1]] = value
        start += value.shape[1]
    width = down_ref.shape[1] - start
    down_ref[:, start:] = total[:, :width]
    up_ref[...] = total[:, width:]


def call(kernel, name, outs, args, far=(), far_outs=(), scratch=(), limit=VMEM_LIMIT):
    def spec(place, places):
        return pl.BlockSpec(memory_space=pltpu.HBM if place in places else pltpu.VMEM)

    return pl.pallas_call(
        kernel,
        in_specs=[spec(i, far) for i in range(len(args))],
        out_specs=[spec(i, far_outs) for i in range(len(outs))],
        out_shape=[jax.ShapeDtypeStruct(shape, kind) for shape, kind in outs],
        scratch_shapes=list(scratch),
        compiler_params=pltpu.CompilerParams(vmem_limit_bytes=limit),
        name=name,
    )(*args)


def body(
    norm_input,
    gain,
    value_weight,
    shrink_factor_matrices,
    expand_factor_matrices,
    value_gradient,
    candidate_index,
    counts,
):
    micro_count, tok_local, features = norm_input.shape[1:]
    n_rows = micro_count * tok_local
    n_cand = counts.shape[0]
    kv_width = value_weight.shape[2]
    n_tensor = lax.axis_size("tensor")
    n_pipe = lax.axis_size("pipe")
    n_dp = lax.axis_size("dp")
    kv_local = kv_width // n_tensor
    n_sel = n_cand * RANK
    wide = features + kv_local
    total_tokens = float(n_rows * n_dp)
    h = norm_input.reshape(n_rows, features)
    shrink = shrink_factor_matrices[0].transpose(0, 2, 1).reshape(n_sel, features)
    expand = expand_factor_matrices.reshape(n_sel, kv_width)
    gradient = value_gradient.reshape(n_rows, kv_width)

    outs = [
        ((n_rows, features), F32),
        ((n_rows, features), BF16),
        ((n_rows, kv_local), BF16),
        ((n_rows, n_sel), F32),
        ((n_rows, n_sel), BF16),
        ((n_rows, 2 * RANK), F32),
    ]
    gained_dn, normed, scaled_part, back, mask, stat = call(
        functools.partial(first_kernel, total_tokens),
        "first",
        outs,
        (candidate_index, counts, h, gain, value_weight[0], shrink, expand, gradient),
        far=range(8),
        far_outs=range(6),
        limit=FIRST_VMEM_LIMIT,
        scratch=[pltpu.VMEM(shape, kind) for shape, kind in outs]
        + [
            pltpu.SMEM(candidate_index.shape, jnp.int32),
            pltpu.SMEM(counts.shape, jnp.int32),
            pltpu.VMEM((n_rows, features), BF16),
            pltpu.VMEM((1, features), F32),
            pltpu.VMEM((features, kv_width), BF16),
            pltpu.VMEM((n_sel, features), BF16),
            pltpu.VMEM((n_sel, kv_width), BF16),
            pltpu.VMEM((n_rows, kv_width), BF16),
            pltpu.VMEM((n_rows, kv_width), BF16),
            pltpu.VMEM((n_rows, n_sel), BF16),
            pltpu.VMEM((n_rows, n_sel), F32),
            pltpu.SemaphoreType.DMA((7 + features // FIRST_BLOCK,)),
            pltpu.SemaphoreType.DMA((4 + 2 * (features // FIRST_BLOCK),)),
        ],
    )

    near = [(i, i ^ 1) for i in range(n_tensor)]
    far = [(i, (i + n_tensor // 2) % n_tensor) for i in range(n_tensor)]
    here = stat + lax.ppermute(stat, "tensor", near)
    there = lax.ppermute(here, "tensor", far)

    quarter = (n_rows // 4, features)
    up, down, first, second = call(
        contrib_kernel,
        "contrib",
        [(quarter, F32)] * 4,
        (here, there, gained_dn, h),
        far=(3,),
        scratch=[pltpu.VMEM((n_rows, features), BF16), pltpu.SemaphoreType.DMA((4,))],
    )
    rise = [(i, (i + 1) % n_pipe) for i in range(n_pipe)]
    fall = [(i, (i - 1) % n_pipe) for i in range(n_pipe)]
    from_below = lax.ppermute(up, "pipe", rise)
    from_above = lax.ppermute(down, "pipe", fall)

    half = n_sel // 2
    ring = n_dp // 2
    widths = (*PART_COLUMNS, wide - sum(PART_COLUMNS) - SWAP_COLUMNS)
    n_parts = len(widths)
    adapter = call(
        adapter_kernel,
        "adapter",
        [((half, width), F32) for width in widths] * 2 + [((2 * RANK, SWAP_COLUMNS), F32)] * ring,
        (here, there, back, mask, normed, scaled_part),
        scratch=[pltpu.VMEM((n_sel, n_rows), BF16)] * 2,
    )
    keep, send = adapter[:n_parts], list(adapter[n_parts : 2 * n_parts])
    swaps = adapter[2 * n_parts :]

    def over(value):
        pairs = [(i, (i + ring) % n_dp) for i in range(n_dp)]
        return lax.ppermute(value, "dp", pairs)

    def across(part):
        return over(send[part])

    def around(part, came):
        out = [((RANK, widths[part]), F32)] * ring
        return turned(call(split_kernel, "split", out, (keep[part], came)))

    def turned(values):
        own, *sends = values
        shares = [own]
        for shift, value in enumerate(sends, 1):
            pairs = [(i, i // ring * ring + (i + shift) % ring) for i in range(n_dp)]
            shares.append(lax.ppermute(value, "dp", pairs))
        return shares

    def summed(part, shares):
        return call(sum_kernel, "sum", [((RANK, widths[part]), F32)], shares)[0]

    groups = n_pipe // 2
    lines = [list(range(first, n_pipe, 2)) for first in range(2)]
    shape = (groups, n_rows // 2 // groups, features)
    came = across(0)
    from_below, from_above, came, send[1], send[2], *swaps = lax.optimization_barrier(
        (from_below, from_above, came, send[1], send[2], *swaps)
    )
    (pair,) = call(pair_kernel, "pair", [(shape, F32)], (first, second, from_below, from_above))
    owned = lax.all_to_all(pair, "pipe", 0, 0, axis_index_groups=lines, tiled=True)
    part_0 = summed(0, around(0, came))
    came = across(1)
    swap_keep, swap_send = call(
        swap_kernel,
        "swap",
        [((RANK, SWAP_COLUMNS), F32)] * 2,
        turned(swaps),
        scratch=[pltpu.VMEM((2 * RANK, SWAP_COLUMNS), F32)],
    )
    owned, part_0, came, send[2], swap_send = lax.optimization_barrier(
        (owned, part_0, came, send[2], swap_send)
    )
    (after,) = call(scan_kernel, "scan", [(shape, F32)], (owned,))
    after = lax.all_to_all(after, "pipe", 0, 0, axis_index_groups=lines, tiled=True)
    part_1 = summed(1, around(1, came))
    came = across(2)
    swap_come = over(swap_send)
    after, part_1, came, swap_come = lax.optimization_barrier((after, part_1, came, swap_come))
    shares = around(2, came)
    rising, falling = call(spread_kernel, "spread", [(quarter, F32)] * 2, (after, first, second))
    last_below = lax.ppermute(rising, "pipe", rise)
    last_above = lax.ppermute(falling, "pipe", fall)
    grad_down, grad_up = call(
        gather_kernel, "gather", [((RANK, features), F32), ((RANK, kv_local), F32)], [part_0, part_1, swap_keep, swap_come, *shares]
    )
    grad_down = grad_down.reshape(1, 1, RANK, features).transpose(0, 1, 3, 2)
    grad_up = grad_up.reshape(1, 1, RANK, kv_local)
    (grad_in,) = call(
        final_kernel,
        "final",
        [((n_rows, features), BF16)],
        (after, up, down, first, second, from_below, from_above, last_below, last_above),
    )
    return grad_in.reshape(1, micro_count, tok_local, features), grad_down, grad_up


def solution(mesh):
    in_specs = (
        P("pipe", None, "dp", "tensor"),
        P("pipe", "tensor"),
        P("pipe", "tensor", None),
        P("pipe", None, "tensor", None),
        P("pipe", None, None, None),
        P("pipe", None, "dp", None),
        P(None, "dp"),
        P(),
    )
    out_specs = (
        P("pipe", None, "dp", "tensor"),
        P("pipe", "dp", "tensor", None),
        P("pipe", "dp", None, "tensor"),
    )
    return jax.shard_map(body, mesh=mesh, in_specs=in_specs, out_specs=out_specs, check_vma=False)
```

profile of v0, /device:TPU:2, one launch (start us, length us, event | category | flops | bytes accessed | tf_op | source)
XLA Modules:
  0.0 117.2 jit_solution(3993270908327380184)
XLA Ops:
  0.6 7.0 %first.1 = (f32[256,2048]{1,0:T(8,128)}, bf16[256,2048]{1,0:T(8,128)(2,1)}, bf16[256,256]{1,0:T(8,128)(2,1)}, f32[256,512]{1,0:T(8,128)}, bf16[256,512]{1,0:T(8,128)(2,1)}, /*index=5*/f32[256,128]{1,0:T(8,128)}) custom-call(s32[4,4]{1,0:T(4,128)} %cand_hbm.1, s32[8]{0:T(128)} %counts_hbm.1, bf16[256,2048]{1,0:T(8,128)(2,1)} %bitcast.14, f32[1,2048]{1,0:T(1,128)} %gain_hbm.1, ...), custom_call_target="tpu_custom_call" | custom-call | tf_op jit(solution)/shard_map/first/pallas_call | solution.py:383
  7.7 1.5 %collective-permute-done = f32[256,128]{1,0:T(8,128)S(1)} collective-permute-done((f32[256,128]{1,0:T(8,128)}, f32[256,128]{1,0:T(8,128)S(1)}, u32[]{:S(2)}, u32[]{:S(2)}) %collective-permute-start) | collective-permute-done | bytes 131104 | tf_op jit(solution)/shard_map/ppermute | solution.py:456
  10.2 2.2 %collective-permute-start.1 = (f32[256,128]{1,0:T(8,128)S(1)}, f32[256,128]{1,0:T(8,128)S(1)}, u32[]{:S(2)}, u32[]{:S(2)}) collective-permute-start(f32[256,128]{1,0:T(8,128)S(1)} %add.3.here_ref), channel_id=1, source_target_pairs={{0,16},{8,24},{16,0},{24,8},{1,17},{9,25},{17,1},{25,9},{2,18},{10... | collective-permute-start | bytes 393224 | tf_op jit(solution)/shard_map/ppermute | solution.py:457
  12.4 4.9 %collective-permute-done.1.there_ref = f32[256,128]{1,0:T(8,128)S(1)} collective-permute-done((f32[256,128]{1,0:T(8,128)S(1)}, f32[256,128]{1,0:T(8,128)S(1)}, u32[]{:S(2)}, u32[]{:S(2)}) %collective-permute-start.1) | collective-permute-done | bytes 131104 | tf_op jit(solution)/shard_map/ppermute | solution.py:457
  18.5 1.6 %copy-done.1 = f32[256,2048]{1,0:T(8,128)S(1)} copy-done((f32[256,2048]{1,0:T(8,128)S(1)}, f32[256,2048]{1,0:T(8,128)}, u32[]{:S(2)}) %copy-start.1) | copy-done | bytes 2097176
  20.9 2.0 %collective-permute-start.2 = (f32[64,2048]{1,0:T(8,128)S(1)}, f32[64,2048]{1,0:T(8,128)S(1)}, u32[]{:S(2)}, u32[]{:S(2)}) collective-permute-start(f32[64,2048]{1,0:T(8,128)S(1)} %get-tuple-element.63.up_ref), channel_id=1, source_target_pairs={{0,32},{32,64},{64,96},{96,128},{128,160},{160,192},{192,224},{224... | collective-permute-start | bytes 1572872 | tf_op jit(solution)/shard_map/ppermute | solution.py:470
  22.9 4.0 %collective-permute-start.3 = (f32[64,2048]{1,0:T(8,128)S(1)}, f32[64,2048]{1,0:T(8,128)S(1)}, u32[]{:S(2)}, u32[]{:S(2)}) collective-permute-start(f32[64,2048]{1,0:T(8,128)S(1)} %get-tuple-element.64.down_ref), channel_id=1, source_target_pairs={{0,224},{32,0},{64,32},{96,64},{128,96},{160,128},{192,160},{224,1... | collective-permute-start | bytes 1572872 | tf_op jit(solution)/shard_map/ppermute | solution.py:471
  32.0 6.7 %collective-permute-done.4.come_ref = f32[256,256]{1,0:T(8,128)S(1)} collective-permute-done((f32[256,256]{1,0:T(8,128)S(1)}, f32[256,256]{1,0:T(8,128)S(1)}, u32[]{:S(2)}, u32[]{:S(2)}) %collective-permute-start.4) | collective-permute-done | bytes 262176 | tf_op jit(solution)/shard_map/ppermute | solution.py:489
  40.6 5.5 %all-to-all-start = ((f32[4,32,2048]{2,1,0:T(8,128)}), f32[4,32,2048]{2,1,0:T(8,128)S(1)}, u32[]{:S(2)}, u32[]{:S(2)}) async-start(f32[4,32,2048]{2,1,0:T(8,128)} %pair.1), calls=%async_computation | async-start | bytes 2097152 | tf_op jit(solution)/shard_map/all_to_all | solution.py:517
  47.6 1.7 %collective-permute-start.5 = (f32[64,256]{1,0:T(8,128)S(1)}, f32[64,256]{1,0:T(8,128)S(1)}, u32[]{:S(2)}, u32[]{:S(2)}) collective-permute-start(f32[64,256]{1,0:T(8,128)S(1)} %get-tuple-element.81), channel_id=1, source_target_pairs={{0,1},{1,2},{2,3},{3,0},{4,5},{5,6},{6,7},{7,4},{8,9},{9,10},{10,1... | collective-permute-start | bytes 196616 | tf_op jit(solution)/shard_map/ppermute | solution.py:503
  49.3 2.9 %collective-permute-start.10 = (f32[128,384]{1,0:T(8,128)}, f32[128,384]{1,0:T(8,128)S(1)}, u32[]{:S(2)}, u32[]{:S(2)}) collective-permute-start(f32[128,384]{1,0:T(8,128)} %copy-done.30), channel_id=1, source_target_pairs={{0,2},{1,3},{2,0},{3,1},{4,6},{5,7},{6,4},{7,5},{8,10},{9,11},{10,... | collective-permute-start | bytes 589832 | tf_op jit(solution)/shard_map/ppermute | solution.py:503
  54.2 2.8 %collective-permute-start.6 = (f32[64,256]{1,0:T(8,128)S(1)}, f32[64,256]{1,0:T(8,128)S(1)}, u32[]{:S(2)}, u32[]{:S(2)}) collective-permute-start(f32[64,256]{1,0:T(8,128)S(1)} %get-tuple-element.82), channel_id=1, source_target_pairs={{0,2},{1,3},{2,0},{3,1},{4,6},{5,7},{6,4},{7,5},{8,10},{9,11},{10,... | collective-permute-start | bytes 196616 | tf_op jit(solution)/shard_map/ppermute | solution.py:503
  57.0 4.4 %collective-permute-done.6.refs_2_ = f32[64,256]{1,0:T(8,128)S(1)} collective-permute-done((f32[64,256]{1,0:T(8,128)S(1)}, f32[64,256]{1,0:T(8,128)S(1)}, u32[]{:S(2)}, u32[]{:S(2)}) %collective-permute-start.6) | collective-permute-done | bytes 65568 | tf_op jit(solution)/shard_map/ppermute | solution.py:503
  62.5 3.1 %collective-permute-done.7.refs_3_ = f32[64,256]{1,0:T(8,128)S(1)} collective-permute-done((f32[64,256]{1,0:T(8,128)S(1)}, f32[64,256]{1,0:T(8,128)S(1)}, u32[]{:S(2)}, u32[]{:S(2)}) %collective-permute-start.7) | collective-permute-done | bytes 65568 | tf_op jit(solution)/shard_map/ppermute | solution.py:503
  71.0 6.9 %all-to-all-start.1 = ((f32[4,32,2048]{2,1,0:T(8,128)}), f32[4,32,2048]{2,1,0:T(8,128)S(1)}, u32[]{:S(2)}, u32[]{:S(2)}) async-start(f32[4,32,2048]{2,1,0:T(8,128)} %scan.1), calls=%async_computation.1 | async-start | bytes 2097152 | tf_op jit(solution)/shard_map/all_to_all | solution.py:531
  81.0 1.6 %collective-permute-start.12 = (f32[64,1024]{1,0:T(8,128)S(1)}, f32[64,1024]{1,0:T(8,128)S(1)}, u32[]{:S(2)}, u32[]{:S(2)}) collective-permute-start(f32[64,1024]{1,0:T(8,128)S(1)} %get-tuple-element.95), channel_id=1, source_target_pairs={{0,1},{1,2},{2,3},{3,0},{4,5},{5,6},{6,7},{7,4},{8,9},{9,10},{10,1... | collective-permute-start | bytes 786440 | tf_op jit(solution)/shard_map/ppermute | solution.py:503
  82.7 2.9 %collective-permute-start.13 = (f32[64,1024]{1,0:T(8,128)S(1)}, f32[64,1024]{1,0:T(8,128)S(1)}, u32[]{:S(2)}, u32[]{:S(2)}) collective-permute-start(f32[64,1024]{1,0:T(8,128)S(1)} %get-tuple-element.96), channel_id=1, source_target_pairs={{0,2},{1,3},{2,0},{3,1},{4,6},{5,7},{6,4},{7,5},{8,10},{9,11},{10,... | collective-permute-start | bytes 786440 | tf_op jit(solution)/shard_map/ppermute | solution.py:503
  88.4 2.7 %collective-permute-done.12.refs_1_ = f32[64,1024]{1,0:T(8,128)S(1)} collective-permute-done((f32[64,1024]{1,0:T(8,128)S(1)}, f32[64,1024]{1,0:T(8,128)S(1)}, u32[]{:S(2)}, u32[]{:S(2)}) %collective-permute-start.12) | collective-permute-done | bytes 262176 | tf_op jit(solution)/shard_map/ppermute | solution.py:503
  91.1 2.8 %collective-permute-done.13.refs_2_ = f32[64,1024]{1,0:T(8,128)S(1)} collective-permute-done((f32[64,1024]{1,0:T(8,128)S(1)}, f32[64,1024]{1,0:T(8,128)S(1)}, u32[]{:S(2)}, u32[]{:S(2)}) %collective-permute-start.13) | collective-permute-done | bytes 262176 | tf_op jit(solution)/shard_map/ppermute | solution.py:503
  95.5 4.5 %all-to-all-done.1.after_ref = f32[4,32,2048]{2,1,0:T(8,128)S(1)} async-done(((f32[4,32,2048]{2,1,0:T(8,128)}), f32[4,32,2048]{2,1,0:T(8,128)S(1)}, u32[]{:S(2)}, u32[]{:S(2)}) %all-to-all-start.1) | async-done | bytes 1048608 | tf_op jit(solution)/shard_map/all_to_all | solution.py:531
  100.3 3.2 %collective-permute-start.18 = (f32[64,2048]{1,0:T(8,128)S(1)}, f32[64,2048]{1,0:T(8,128)S(1)}, u32[]{:S(2)}, u32[]{:S(2)}) collective-permute-start(f32[64,2048]{1,0:T(8,128)S(1)} %get-tuple-element.102), channel_id=1, source_target_pairs={{0,224},{32,0},{64,32},{96,64},{128,96},{160,128},{192,160},{224,1... | collective-permute-start | bytes 1572872 | tf_op jit(solution)/shard_map/ppermute | solution.py:539
  103.6 1.6 %collective-permute-start.19 = (f32[64,640]{1,0:T(8,128)S(1)}, f32[64,640]{1,0:T(8,128)S(1)}, u32[]{:S(2)}, u32[]{:S(2)}) collective-permute-start(f32[64,640]{1,0:T(8,128)S(1)} %get-tuple-element.110), channel_id=1, source_target_pairs={{0,1},{1,2},{2,3},{3,0},{4,5},{5,6},{6,7},{7,4},{8,9},{9,10},{10,1... | collective-permute-start | bytes 491528 | tf_op jit(solution)/shard_map/ppermute | solution.py:503
  105.2 2.9 %collective-permute-start.20 = (f32[64,640]{1,0:T(8,128)S(1)}, f32[64,640]{1,0:T(8,128)S(1)}, u32[]{:S(2)}, u32[]{:S(2)}) collective-permute-start(f32[64,640]{1,0:T(8,128)S(1)} %get-tuple-element.111), channel_id=1, source_target_pairs={{0,2},{1,3},{2,0},{3,1},{4,6},{5,7},{6,4},{7,5},{8,10},{9,11},{10,... | collective-permute-start | bytes 491528 | tf_op jit(solution)/shard_map/ppermute | solution.py:503
  110.8 4.3 %collective-permute-done.20.refs_2_ = f32[64,640]{1,0:T(8,128)S(1)} collective-permute-done((f32[64,640]{1,0:T(8,128)S(1)}, f32[64,640]{1,0:T(8,128)S(1)}, u32[]{:S(2)}, u32[]{:S(2)}) %collective-permute-start.20) | collective-permute-done | bytes 163872 | tf_op jit(solution)/shard_map/ppermute | solution.py:503
  (103 shorter events, 32.5 us)
Async XLA Ops:
  7.6 1.6 %collective-permute-start = (f32[256,128]{1,0:T(8,128)}, f32[256,128]{1,0:T(8,128)S(1)}, u32[]{:S(2)}, u32[]{:S(2)}) collective-permute-start(f32[256,128]{1,0:T(8,128)} %get-tuple-element.59), channel_id=1, source_target_pairs={{0,8},{8,0},{16,24},{24,16},{1,9},{9,1},{17,25},{25,17},{2,10},{10... | collective-permute-start | bytes 393224 | tf_op jit(solution)/shard_map/ppermute | solution.py:456
  10.2 7.1 %collective-permute-start.1 = (f32[256,128]{1,0:T(8,128)S(1)}, f32[256,128]{1,0:T(8,128)S(1)}, u32[]{:S(2)}, u32[]{:S(2)}) collective-permute-start(f32[256,128]{1,0:T(8,128)S(1)} %add.3.here_ref), channel_id=1, source_target_pairs={{0,16},{8,24},{16,0},{24,8},{1,17},{9,25},{17,1},{25,9},{2,18},{10... | collective-permute-start | bytes 393224 | tf_op jit(solution)/shard_map/ppermute | solution.py:457
  20.9 18.5 %collective-permute-start.2 = (f32[64,2048]{1,0:T(8,128)S(1)}, f32[64,2048]{1,0:T(8,128)S(1)}, u32[]{:S(2)}, u32[]{:S(2)}) collective-permute-start(f32[64,2048]{1,0:T(8,128)S(1)} %get-tuple-element.63.up_ref), channel_id=1, source_target_pairs={{0,32},{32,64},{64,96},{96,128},{128,160},{160,192},{192,224},{224... | collective-permute-start | bytes 1572872 | tf_op jit(solution)/shard_map/ppermute | solution.py:470
  22.9 16.5 %collective-permute-start.3 = (f32[64,2048]{1,0:T(8,128)S(1)}, f32[64,2048]{1,0:T(8,128)S(1)}, u32[]{:S(2)}, u32[]{:S(2)}) collective-permute-start(f32[64,2048]{1,0:T(8,128)S(1)} %get-tuple-element.64.down_ref), channel_id=1, source_target_pairs={{0,224},{32,0},{64,32},{96,64},{128,96},{160,128},{192,160},{224,1... | collective-permute-start | bytes 1572872 | tf_op jit(solution)/shard_map/ppermute | solution.py:471
  31.4 7.3 %collective-permute-start.4 = (f32[256,256]{1,0:T(8,128)S(1)}, f32[256,256]{1,0:T(8,128)S(1)}, u32[]{:S(2)}, u32[]{:S(2)}) collective-permute-start(f32[256,256]{1,0:T(8,128)S(1)} %get-tuple-element.69), channel_id=1, source_target_pairs={{0,4},{1,5},{2,6},{3,7},{4,0},{5,1},{6,2},{7,3},{8,12},{9,13},{10,... | collective-permute-start | bytes 786440 | tf_op jit(solution)/shard_map/ppermute | solution.py:489
  40.6 29.3 %all-to-all-start = ((f32[4,32,2048]{2,1,0:T(8,128)}), f32[4,32,2048]{2,1,0:T(8,128)S(1)}, u32[]{:S(2)}, u32[]{:S(2)}) async-start(f32[4,32,2048]{2,1,0:T(8,128)} %pair.1), calls=%async_computation | async-start | bytes 2097152 | tf_op jit(solution)/shard_map/all_to_all | solution.py:517
  46.1 22.8 %collective-permute-start.8 = (f32[256,1024]{1,0:T(8,128)}, f32[256,1024]{1,0:T(8,128)S(1)}, u32[]{:S(2)}, u32[]{:S(2)}) collective-permute-start(f32[256,1024]{1,0:T(8,128)} %copy-done.26), channel_id=1, source_target_pairs={{0,4},{1,5},{2,6},{3,7},{4,0},{5,1},{6,2},{7,3},{8,12},{9,13},{10,... | collective-permute-start | bytes 3145736 | tf_op jit(solution)/shard_map/ppermute | solution.py:489
  47.6 6.6 %collective-permute-start.5 = (f32[64,256]{1,0:T(8,128)S(1)}, f32[64,256]{1,0:T(8,128)S(1)}, u32[]{:S(2)}, u32[]{:S(2)}) collective-permute-start(f32[64,256]{1,0:T(8,128)S(1)} %get-tuple-element.81), channel_id=1, source_target_pairs={{0,1},{1,2},{2,3},{3,0},{4,5},{5,6},{6,7},{7,4},{8,9},{9,10},{10,1... | collective-permute-start | bytes 196616 | tf_op jit(solution)/shard_map/ppermute | solution.py:503
  49.3 16.4 %collective-permute-start.10 = (f32[128,384]{1,0:T(8,128)}, f32[128,384]{1,0:T(8,128)S(1)}, u32[]{:S(2)}, u32[]{:S(2)}) collective-permute-start(f32[128,384]{1,0:T(8,128)} %copy-done.30), channel_id=1, source_target_pairs={{0,2},{1,3},{2,0},{3,1},{4,6},{5,7},{6,4},{7,5},{8,10},{9,11},{10,... | collective-permute-start | bytes 589832 | tf_op jit(solution)/shard_map/ppermute | solution.py:503
  52.2 13.5 %collective-permute-start.11 = (f32[128,384]{1,0:T(8,128)}, f32[128,384]{1,0:T(8,128)S(1)}, u32[]{:S(2)}, u32[]{:S(2)}) collective-permute-start(f32[128,384]{1,0:T(8,128)} %copy-done.29), channel_id=1, source_target_pairs={{0,3},{1,0},{2,1},{3,2},{4,7},{5,4},{6,5},{7,6},{8,11},{9,8},{10,9... | collective-permute-start | bytes 589832 | tf_op jit(solution)/shard_map/ppermute | solution.py:503
  53.5 12.2 %collective-permute-start.9 = (f32[128,384]{1,0:T(8,128)}, f32[128,384]{1,0:T(8,128)S(1)}, u32[]{:S(2)}, u32[]{:S(2)}) collective-permute-start(f32[128,384]{1,0:T(8,128)} %copy-done.28), channel_id=1, source_target_pairs={{0,1},{1,2},{2,3},{3,0},{4,5},{5,6},{6,7},{7,4},{8,9},{9,10},{10,1... | collective-permute-start | bytes 589832 | tf_op jit(solution)/shard_map/ppermute | solution.py:503
  54.2 7.2 %collective-permute-start.6 = (f32[64,256]{1,0:T(8,128)S(1)}, f32[64,256]{1,0:T(8,128)S(1)}, u32[]{:S(2)}, u32[]{:S(2)}) collective-permute-start(f32[64,256]{1,0:T(8,128)S(1)} %get-tuple-element.82), channel_id=1, source_target_pairs={{0,2},{1,3},{2,0},{3,1},{4,6},{5,7},{6,4},{7,5},{8,10},{9,11},{10,... | collective-permute-start | bytes 196616 | tf_op jit(solution)/shard_map/ppermute | solution.py:503
  61.4 4.3 %collective-permute-start.7 = (f32[64,256]{1,0:T(8,128)S(1)}, f32[64,256]{1,0:T(8,128)S(1)}, u32[]{:S(2)}, u32[]{:S(2)}) collective-permute-start(f32[64,256]{1,0:T(8,128)S(1)} %get-tuple-element.83), channel_id=1, source_target_pairs={{0,3},{1,0},{2,1},{3,2},{4,7},{5,4},{6,5},{7,6},{8,11},{9,8},{10,9... | collective-permute-start | bytes 196616 | tf_op jit(solution)/shard_map/ppermute | solution.py:503
  71.0 29.0 %all-to-all-start.1 = ((f32[4,32,2048]{2,1,0:T(8,128)}), f32[4,32,2048]{2,1,0:T(8,128)S(1)}, u32[]{:S(2)}, u32[]{:S(2)}) async-start(f32[4,32,2048]{2,1,0:T(8,128)} %scan.1), calls=%async_computation.1 | async-start | bytes 2097152 | tf_op jit(solution)/shard_map/all_to_all | solution.py:531
  77.9 16.7 %collective-permute-start.15 = (f32[256,640]{1,0:T(8,128)}, f32[256,640]{1,0:T(8,128)S(1)}, u32[]{:S(2)}, u32[]{:S(2)}) collective-permute-start(f32[256,640]{1,0:T(8,128)} %copy-done.27), channel_id=1, source_target_pairs={{0,4},{1,5},{2,6},{3,7},{4,0},{5,1},{6,2},{7,3},{8,12},{9,13},{10,... | collective-permute-start | bytes 1966088 | tf_op jit(solution)/shard_map/ppermute | solution.py:489
  81.0 10.1 %collective-permute-start.12 = (f32[64,1024]{1,0:T(8,128)S(1)}, f32[64,1024]{1,0:T(8,128)S(1)}, u32[]{:S(2)}, u32[]{:S(2)}) collective-permute-start(f32[64,1024]{1,0:T(8,128)S(1)} %get-tuple-element.95), channel_id=1, source_target_pairs={{0,1},{1,2},{2,3},{3,0},{4,5},{5,6},{6,7},{7,4},{8,9},{9,10},{10,1... | collective-permute-start | bytes 786440 | tf_op jit(solution)/shard_map/ppermute | solution.py:503
  82.7 11.2 %collective-permute-start.13 = (f32[64,1024]{1,0:T(8,128)S(1)}, f32[64,1024]{1,0:T(8,128)S(1)}, u32[]{:S(2)}, u32[]{:S(2)}) collective-permute-start(f32[64,1024]{1,0:T(8,128)S(1)} %get-tuple-element.96), channel_id=1, source_target_pairs={{0,2},{1,3},{2,0},{3,1},{4,6},{5,7},{6,4},{7,5},{8,10},{9,11},{10,... | collective-permute-start | bytes 786440 | tf_op jit(solution)/shard_map/ppermute | solution.py:503
  85.6 8.3 %collective-permute-start.14 = (f32[64,1024]{1,0:T(8,128)S(1)}, f32[64,1024]{1,0:T(8,128)S(1)}, u32[]{:S(2)}, u32[]{:S(2)}) collective-permute-start(f32[64,1024]{1,0:T(8,128)S(1)} %get-tuple-element.97), channel_id=1, source_target_pairs={{0,3},{1,0},{2,1},{3,2},{4,7},{5,4},{6,5},{7,6},{8,11},{9,8},{10,9... | collective-permute-start | bytes 786440 | tf_op jit(solution)/shard_map/ppermute | solution.py:503
  86.9 7.1 %collective-permute-start.16 = (f32[64,384]{1,0:T(8,128)}, f32[64,384]{1,0:T(8,128)S(1)}, u32[]{:S(2)}, u32[]{:S(2)}) collective-permute-start(f32[64,384]{1,0:T(8,128)} %copy-done.31), channel_id=1, source_target_pairs={{0,4},{1,5},{2,6},{3,7},{4,0},{5,1},{6,2},{7,3},{8,12},{9,13},{10,... | collective-permute-start | bytes 294920 | tf_op jit(solution)/shard_map/ppermute | solution.py:489
  100.2 15.8 %collective-permute-start.17 = (f32[64,2048]{1,0:T(8,128)S(1)}, f32[64,2048]{1,0:T(8,128)S(1)}, u32[]{:S(2)}, u32[]{:S(2)}) collective-permute-start(f32[64,2048]{1,0:T(8,128)S(1)} %get-tuple-element.101), channel_id=1, source_target_pairs={{0,32},{32,64},{64,96},{96,128},{128,160},{160,192},{192,224},{224... | collective-permute-start | bytes 1572872 | tf_op jit(solution)/shard_map/ppermute | solution.py:538
  100.3 15.7 %collective-permute-start.18 = (f32[64,2048]{1,0:T(8,128)S(1)}, f32[64,2048]{1,0:T(8,128)S(1)}, u32[]{:S(2)}, u32[]{:S(2)}) collective-permute-start(f32[64,2048]{1,0:T(8,128)S(1)} %get-tuple-element.102), channel_id=1, source_target_pairs={{0,224},{32,0},{64,32},{96,64},{128,96},{160,128},{192,160},{224,1... | collective-permute-start | bytes 1572872 | tf_op jit(solution)/shard_map/ppermute | solution.py:539
  103.6 7.2 %collective-permute-start.19 = (f32[64,640]{1,0:T(8,128)S(1)}, f32[64,640]{1,0:T(8,128)S(1)}, u32[]{:S(2)}, u32[]{:S(2)}) collective-permute-start(f32[64,640]{1,0:T(8,128)S(1)} %get-tuple-element.110), channel_id=1, source_target_pairs={{0,1},{1,2},{2,3},{3,0},{4,5},{5,6},{6,7},{7,4},{8,9},{9,10},{10,1... | collective-permute-start | bytes 491528 | tf_op jit(solution)/shard_map/ppermute | solution.py:503
  105.2 9.9 %collective-permute-start.20 = (f32[64,640]{1,0:T(8,128)S(1)}, f32[64,640]{1,0:T(8,128)S(1)}, u32[]{:S(2)}, u32[]{:S(2)}) collective-permute-start(f32[64,640]{1,0:T(8,128)S(1)} %get-tuple-element.111), channel_id=1, source_target_pairs={{0,2},{1,3},{2,0},{3,1},{4,6},{5,7},{6,4},{7,5},{8,10},{9,11},{10,... | collective-permute-start | bytes 491528 | tf_op jit(solution)/shard_map/ppermute | solution.py:503
  108.0 7.0 %collective-permute-start.21 = (f32[64,640]{1,0:T(8,128)S(1)}, f32[64,640]{1,0:T(8,128)S(1)}, u32[]{:S(2)}, u32[]{:S(2)}) collective-permute-start(f32[64,640]{1,0:T(8,128)S(1)} %get-tuple-element.112), channel_id=1, source_target_pairs={{0,3},{1,0},{2,1},{3,2},{4,7},{5,4},{6,5},{7,6},{8,11},{9,8},{10,9... | collective-permute-start | bytes 491528 | tf_op jit(solution)/shard_map/ppermute | solution.py:503
  (32 other events, 205.7 us)
where the time goes:
time: 118 us; the launch traced here: 117 us
  starting transfers between devices  49.5 us (42%)
  waiting for transfers between devices  37.3 us (32%)
  local copies, waits for them, and re-layouts  15 us (13%)
  Pallas kernels  13.6 us (12%)
    ppermute x12, starting transfers between devices, turned(): shares.append(lax.ppermute(value, 'dp', pairs))  22.3 us
    ppermute x12, waiting for transfers between devices, turned(): shares.append(lax.ppermute(value, 'dp', pairs))  18.7 us
    unnamed x64, local copies, waits for them, and re-layouts  15 us
    pallas_call x14, Pallas kernels, call(): pl.pallas_call(kernel, in_specs=[spec(i, far) for i in range(len(args))],...  13.6 us
    ppermute x4, waiting for transfers between devices, over(): return lax.ppermute(value, 'dp', pairs)  7.66 us
    all_to_all x1, starting transfers between devices, body(): lax.all_to_all(after, 'pipe', 0, 0, axis_index_groups=lines, tiled=True)  6.92 us
    all_to_all x1, starting transfers between devices, body(): lax.all_to_all(pair, 'pipe', 0, 0, axis_index_groups=lines, tiled=True)  5.46 us
    ppermute x1, waiting for transfers between devices, body(): there = lax.ppermute(here, 'tensor', far)  4.94 us
  transfers between devices with their start and end apart: 24, of which 11 were waited for; matrix products, arithmetic and copies ran while one was open for 0% of the time, Pallas kernels for 2%

commit v1 on v0

--- a/solution.py
+++ b/solution.py
@@ -16,7 +16,7 @@
 PART_COLUMNS = (256, 1024)
 SWAP_COLUMNS = 384
 VMEM_LIMIT = 16 * 1024 * 1024
-FIRST_VMEM_LIMIT = 64 * 1024 * 1024
+FIRST_VMEM_LIMIT = 62 * 1024 * 1024
 NT = (((1,), (1,)), ((), ()))
 NN = (((1,), (0,)), ((), ()))
 F32 = jnp.float32

time: 118 us -> 116 us (0.983)
  local copies, waits for them, and re-layouts: 15 us -> 13.7 us
    unnamed x64, local copies, waits for them, and re-layouts: 15 us -> 13.7 us
where the time goes in v1:
time: 116 us
  starting transfers between devices  49.6 us (43%)
  waiting for transfers between devices  37.3 us (32%)
  local copies, waits for them, and re-layouts  13.7 us (12%)
  Pallas kernels  13.6 us (12%)
    ppermute x12, starting transfers between devices, turned(): shares.append(lax.ppermute(value, 'dp', pairs))  22.4 us
    ppermute x12, waiting for transfers between devices, turned(): shares.append(lax.ppermute(value, 'dp', pairs))  18.7 us
    unnamed x64, local copies, waits for them, and re-layouts  13.7 us
    pallas_call x14, Pallas kernels, call(): pl.pallas_call(kernel, in_specs=[spec(i, far) for i in range(len(args))],...  13.6 us
    ppermute x4, waiting for transfers between devices, over(): return lax.ppermute(value, 'dp', pairs)  7.64 us
    all_to_all x1, starting transfers between devices, body(): lax.all_to_all(after, 'pipe', 0, 0, axis_index_groups=lines, tiled=True)  6.92 us
    all_to_all x1, starting transfers between devices, body(): lax.all_to_all(pair, 'pipe', 0, 0, axis_index_groups=lines, tiled=True)  5.47 us
    ppermute x1, waiting for transfers between devices, body(): there = lax.ppermute(here, 'tensor', far)  4.93 us
  transfers between devices with their start and end apart: 24, of which 11 were waited for; matrix products, arithmetic and copies ran while one was open for 0% of the time, Pallas kernels for 2%

profile of v1, /device:TPU:2, one launch (start us, length us, event | category | flops | bytes accessed | tf_op | source)
XLA Modules:
  0.0 116.0 jit_solution(17519805255125109408)
XLA Ops:
  0.6 7.0 %first.1 = (f32[256,2048]{1,0:T(8,128)}, bf16[256,2048]{1,0:T(8,128)(2,1)}, bf16[256,256]{1,0:T(8,128)(2,1)}, f32[256,512]{1,0:T(8,128)}, bf16[256,512]{1,0:T(8,128)(2,1)}, /*index=5*/f32[256,128]{1,0:T(8,128)}) custom-call(s32[4,4]{1,0:T(4,128)} %cand_hbm.1, s32[8]{0:T(128)} %counts_hbm.1, bf16[256,2048]{1,0:T(8,128)(2,1)} %bitcast.14, f32[1,2048]{1,0:T(1,128)} %gain_hbm.1, ...), custom_call_target="tpu_custom_call" | custom-call | tf_op jit(solution)/shard_map/first/pallas_call | solution.py:383
  7.8 1.5 %collective-permute-done = f32[256,128]{1,0:T(8,128)S(1)} collective-permute-done((f32[256,128]{1,0:T(8,128)}, f32[256,128]{1,0:T(8,128)S(1)}, u32[]{:S(2)}, u32[]{:S(2)}) %collective-permute-start) | collective-permute-done | bytes 131104 | tf_op jit(solution)/shard_map/ppermute | solution.py:456
  10.2 2.2 %collective-permute-start.1 = (f32[256,128]{1,0:T(8,128)S(1)}, f32[256,128]{1,0:T(8,128)S(1)}, u32[]{:S(2)}, u32[]{:S(2)}) collective-permute-start(f32[256,128]{1,0:T(8,128)S(1)} %add.3.here_ref), channel_id=1, source_target_pairs={{0,16},{8,24},{16,0},{24,8},{1,17},{9,25},{17,1},{25,9},{2,18},{10... | collective-permute-start | bytes 393224 | tf_op jit(solution)/shard_map/ppermute | solution.py:457
  12.5 4.9 %collective-permute-done.1.there_ref = f32[256,128]{1,0:T(8,128)S(1)} collective-permute-done((f32[256,128]{1,0:T(8,128)S(1)}, f32[256,128]{1,0:T(8,128)S(1)}, u32[]{:S(2)}, u32[]{:S(2)}) %collective-permute-start.1) | collective-permute-done | bytes 131104 | tf_op jit(solution)/shard_map/ppermute | solution.py:457
  17.4 1.6 %copy-done.1 = f32[256,2048]{1,0:T(8,128)S(1)} copy-done((f32[256,2048]{1,0:T(8,128)S(1)}, f32[256,2048]{1,0:T(8,128)}, u32[]{:S(2)}) %copy-start.1) | copy-done | bytes 2097176
  19.8 2.0 %collective-permute-start.2 = (f32[64,2048]{1,0:T(8,128)S(1)}, f32[64,2048]{1,0:T(8,128)S(1)}, u32[]{:S(2)}, u32[]{:S(2)}) collective-permute-start(f32[64,2048]{1,0:T(8,128)S(1)} %get-tuple-element.63.up_ref), channel_id=1, source_target_pairs={{0,32},{32,64},{64,96},{96,128},{128,160},{160,192},{192,224},{224... | collective-permute-start | bytes 1572872 | tf_op jit(solution)/shard_map/ppermute | solution.py:470
  21.8 4.0 %collective-permute-start.3 = (f32[64,2048]{1,0:T(8,128)S(1)}, f32[64,2048]{1,0:T(8,128)S(1)}, u32[]{:S(2)}, u32[]{:S(2)}) collective-permute-start(f32[64,2048]{1,0:T(8,128)S(1)} %get-tuple-element.64.down_ref), channel_id=1, source_target_pairs={{0,224},{32,0},{64,32},{96,64},{128,96},{160,128},{192,160},{224,1... | collective-permute-start | bytes 1572872 | tf_op jit(solution)/shard_map/ppermute | solution.py:471
  30.9 6.7 %collective-permute-done.4.come_ref = f32[256,256]{1,0:T(8,128)S(1)} collective-permute-done((f32[256,256]{1,0:T(8,128)S(1)}, f32[256,256]{1,0:T(8,128)S(1)}, u32[]{:S(2)}, u32[]{:S(2)}) %collective-permute-start.4) | collective-permute-done | bytes 262176 | tf_op jit(solution)/shard_map/ppermute | solution.py:489
  39.5 5.5 %all-to-all-start = ((f32[4,32,2048]{2,1,0:T(8,128)}), f32[4,32,2048]{2,1,0:T(8,128)S(1)}, u32[]{:S(2)}, u32[]{:S(2)}) async-start(f32[4,32,2048]{2,1,0:T(8,128)} %pair.1), calls=%async_computation | async-start | bytes 2097152 | tf_op jit(solution)/shard_map/all_to_all | solution.py:517
  46.5 1.6 %collective-permute-start.5 = (f32[64,256]{1,0:T(8,128)S(1)}, f32[64,256]{1,0:T(8,128)S(1)}, u32[]{:S(2)}, u32[]{:S(2)}) collective-permute-start(f32[64,256]{1,0:T(8,128)S(1)} %get-tuple-element.81), channel_id=1, source_target_pairs={{0,1},{1,2},{2,3},{3,0},{4,5},{5,6},{6,7},{7,4},{8,9},{9,10},{10,1... | collective-permute-start | bytes 196616 | tf_op jit(solution)/shard_map/ppermute | solution.py:503
  48.1 2.9 %collective-permute-start.10 = (f32[128,384]{1,0:T(8,128)}, f32[128,384]{1,0:T(8,128)S(1)}, u32[]{:S(2)}, u32[]{:S(2)}) collective-permute-start(f32[128,384]{1,0:T(8,128)} %copy-done.30), channel_id=1, source_target_pairs={{0,2},{1,3},{2,0},{3,1},{4,6},{5,7},{6,4},{7,5},{8,10},{9,11},{10,... | collective-permute-start | bytes 589832 | tf_op jit(solution)/shard_map/ppermute | solution.py:503
  53.0 2.8 %collective-permute-start.6 = (f32[64,256]{1,0:T(8,128)S(1)}, f32[64,256]{1,0:T(8,128)S(1)}, u32[]{:S(2)}, u32[]{:S(2)}) collective-permute-start(f32[64,256]{1,0:T(8,128)S(1)} %get-tuple-element.82), channel_id=1, source_target_pairs={{0,2},{1,3},{2,0},{3,1},{4,6},{5,7},{6,4},{7,5},{8,10},{9,11},{10,... | collective-permute-start | bytes 196616 | tf_op jit(solution)/shard_map/ppermute | solution.py:503
  55.9 4.3 %collective-permute-done.6.refs_2_ = f32[64,256]{1,0:T(8,128)S(1)} collective-permute-done((f32[64,256]{1,0:T(8,128)S(1)}, f32[64,256]{1,0:T(8,128)S(1)}, u32[]{:S(2)}, u32[]{:S(2)}) %collective-permute-start.6) | collective-permute-done | bytes 65568 | tf_op jit(solution)/shard_map/ppermute | solution.py:503
  61.4 3.1 %collective-permute-done.7.refs_3_ = f32[64,256]{1,0:T(8,128)S(1)} collective-permute-done((f32[64,256]{1,0:T(8,128)S(1)}, f32[64,256]{1,0:T(8,128)S(1)}, u32[]{:S(2)}, u32[]{:S(2)}) %collective-permute-start.7) | collective-permute-done | bytes 65568 | tf_op jit(solution)/shard_map/ppermute | solution.py:503
  69.8 6.9 %all-to-all-start.1 = ((f32[4,32,2048]{2,1,0:T(8,128)}), f32[4,32,2048]{2,1,0:T(8,128)S(1)}, u32[]{:S(2)}, u32[]{:S(2)}) async-start(f32[4,32,2048]{2,1,0:T(8,128)} %scan.1), calls=%async_computation.1 | async-start | bytes 2097152 | tf_op jit(solution)/shard_map/all_to_all | solution.py:531
  79.9 1.6 %collective-permute-start.12 = (f32[64,1024]{1,0:T(8,128)S(1)}, f32[64,1024]{1,0:T(8,128)S(1)}, u32[]{:S(2)}, u32[]{:S(2)}) collective-permute-start(f32[64,1024]{1,0:T(8,128)S(1)} %get-tuple-element.95), channel_id=1, source_target_pairs={{0,1},{1,2},{2,3},{3,0},{4,5},{5,6},{6,7},{7,4},{8,9},{9,10},{10,1... | collective-permute-start | bytes 786440 | tf_op jit(solution)/shard_map/ppermute | solution.py:503
  81.5 2.9 %collective-permute-start.13 = (f32[64,1024]{1,0:T(8,128)S(1)}, f32[64,1024]{1,0:T(8,128)S(1)}, u32[]{:S(2)}, u32[]{:S(2)}) collective-permute-start(f32[64,1024]{1,0:T(8,128)S(1)} %get-tuple-element.96), channel_id=1, source_target_pairs={{0,2},{1,3},{2,0},{3,1},{4,6},{5,7},{6,4},{7,5},{8,10},{9,11},{10,... | collective-permute-start | bytes 786440 | tf_op jit(solution)/shard_map/ppermute | solution.py:503
  87.2 2.7 %collective-permute-done.12.refs_1_ = f32[64,1024]{1,0:T(8,128)S(1)} collective-permute-done((f32[64,1024]{1,0:T(8,128)S(1)}, f32[64,1024]{1,0:T(8,128)S(1)}, u32[]{:S(2)}, u32[]{:S(2)}) %collective-permute-start.12) | collective-permute-done | bytes 262176 | tf_op jit(solution)/shard_map/ppermute | solution.py:503
  90.0 2.8 %collective-permute-done.13.refs_2_ = f32[64,1024]{1,0:T(8,128)S(1)} collective-permute-done((f32[64,1024]{1,0:T(8,128)S(1)}, f32[64,1024]{1,0:T(8,128)S(1)}, u32[]{:S(2)}, u32[]{:S(2)}) %collective-permute-start.13) | collective-permute-done | bytes 262176 | tf_op jit(solution)/shard_map/ppermute | solution.py:503
  94.4 4.4 %all-to-all-done.1.after_ref = f32[4,32,2048]{2,1,0:T(8,128)S(1)} async-done(((f32[4,32,2048]{2,1,0:T(8,128)}), f32[4,32,2048]{2,1,0:T(8,128)S(1)}, u32[]{:S(2)}, u32[]{:S(2)}) %all-to-all-start.1) | async-done | bytes 1048608 | tf_op jit(solution)/shard_map/all_to_all | solution.py:531
  99.1 3.2 %collective-permute-start.18 = (f32[64,2048]{1,0:T(8,128)S(1)}, f32[64,2048]{1,0:T(8,128)S(1)}, u32[]{:S(2)}, u32[]{:S(2)}) collective-permute-start(f32[64,2048]{1,0:T(8,128)S(1)} %get-tuple-element.102), channel_id=1, source_target_pairs={{0,224},{32,0},{64,32},{96,64},{128,96},{160,128},{192,160},{224,1... | collective-permute-start | bytes 1572872 | tf_op jit(solution)/shard_map/ppermute | solution.py:539
  102.4 1.7 %collective-permute-start.19 = (f32[64,640]{1,0:T(8,128)S(1)}, f32[64,640]{1,0:T(8,128)S(1)}, u32[]{:S(2)}, u32[]{:S(2)}) collective-permute-start(f32[64,640]{1,0:T(8,128)S(1)} %get-tuple-element.110), channel_id=1, source_target_pairs={{0,1},{1,2},{2,3},{3,0},{4,5},{5,6},{6,7},{7,4},{8,9},{9,10},{10,1... | collective-permute-start | bytes 491528 | tf_op jit(solution)/shard_map/ppermute | solution.py:503
  104.0 2.9 %collective-permute-start.20 = (f32[64,640]{1,0:T(8,128)S(1)}, f32[64,640]{1,0:T(8,128)S(1)}, u32[]{:S(2)}, u32[]{:S(2)}) collective-permute-start(f32[64,640]{1,0:T(8,128)S(1)} %get-tuple-element.111), channel_id=1, source_target_pairs={{0,2},{1,3},{2,0},{3,1},{4,6},{5,7},{6,4},{7,5},{8,10},{9,11},{10,... | collective-permute-start | bytes 491528 | tf_op jit(solution)/shard_map/ppermute | solution.py:503
  109.7 4.3 %collective-permute-done.20.refs_2_ = f32[64,640]{1,0:T(8,128)S(1)} collective-permute-done((f32[64,640]{1,0:T(8,128)S(1)}, f32[64,640]{1,0:T(8,128)S(1)}, u32[]{:S(2)}, u32[]{:S(2)}) %collective-permute-start.20) | collective-permute-done | bytes 163872 | tf_op jit(solution)/shard_map/ppermute | solution.py:503
  (103 shorter events, 31.3 us)
Async XLA Ops:
  7.7 1.6 %collective-permute-start = (f32[256,128]{1,0:T(8,128)}, f32[256,128]{1,0:T(8,128)S(1)}, u32[]{:S(2)}, u32[]{:S(2)}) collective-permute-start(f32[256,128]{1,0:T(8,128)} %get-tuple-element.59), channel_id=1, source_target_pairs={{0,8},{8,0},{16,24},{24,16},{1,9},{9,1},{17,25},{25,17},{2,10},{10... | collective-permute-start | bytes 393224 | tf_op jit(solution)/shard_map/ppermute | solution.py:456
  10.2 7.1 %collective-permute-start.1 = (f32[256,128]{1,0:T(8,128)S(1)}, f32[256,128]{1,0:T(8,128)S(1)}, u32[]{:S(2)}, u32[]{:S(2)}) collective-permute-start(f32[256,128]{1,0:T(8,128)S(1)} %add.3.here_ref), channel_id=1, source_target_pairs={{0,16},{8,24},{16,0},{24,8},{1,17},{9,25},{17,1},{25,9},{2,18},{10... | collective-permute-start | bytes 393224 | tf_op jit(solution)/shard_map/ppermute | solution.py:457
  19.8 18.5 %collective-permute-start.2 = (f32[64,2048]{1,0:T(8,128)S(1)}, f32[64,2048]{1,0:T(8,128)S(1)}, u32[]{:S(2)}, u32[]{:S(2)}) collective-permute-start(f32[64,2048]{1,0:T(8,128)S(1)} %get-tuple-element.63.up_ref), channel_id=1, source_target_pairs={{0,32},{32,64},{64,96},{96,128},{128,160},{160,192},{192,224},{224... | collective-permute-start | bytes 1572872 | tf_op jit(solution)/shard_map/ppermute | solution.py:470
  21.8 16.5 %collective-permute-start.3 = (f32[64,2048]{1,0:T(8,128)S(1)}, f32[64,2048]{1,0:T(8,128)S(1)}, u32[]{:S(2)}, u32[]{:S(2)}) collective-permute-start(f32[64,2048]{1,0:T(8,128)S(1)} %get-tuple-element.64.down_ref), channel_id=1, source_target_pairs={{0,224},{32,0},{64,32},{96,64},{128,96},{160,128},{192,160},{224,1... | collective-permute-start | bytes 1572872 | tf_op jit(solution)/shard_map/ppermute | solution.py:471
  30.2 7.3 %collective-permute-start.4 = (f32[256,256]{1,0:T(8,128)S(1)}, f32[256,256]{1,0:T(8,128)S(1)}, u32[]{:S(2)}, u32[]{:S(2)}) collective-permute-start(f32[256,256]{1,0:T(8,128)S(1)} %get-tuple-element.69), channel_id=1, source_target_pairs={{0,4},{1,5},{2,6},{3,7},{4,0},{5,1},{6,2},{7,3},{8,12},{9,13},{10,... | collective-permute-start | bytes 786440 | tf_op jit(solution)/shard_map/ppermute | solution.py:489
  39.5 29.3 %all-to-all-start = ((f32[4,32,2048]{2,1,0:T(8,128)}), f32[4,32,2048]{2,1,0:T(8,128)S(1)}, u32[]{:S(2)}, u32[]{:S(2)}) async-start(f32[4,32,2048]{2,1,0:T(8,128)} %pair.1), calls=%async_computation | async-start | bytes 2097152 | tf_op jit(solution)/shard_map/all_to_all | solution.py:517
  44.9 22.8 %collective-permute-start.8 = (f32[256,1024]{1,0:T(8,128)}, f32[256,1024]{1,0:T(8,128)S(1)}, u32[]{:S(2)}, u32[]{:S(2)}) collective-permute-start(f32[256,1024]{1,0:T(8,128)} %copy-done.26), channel_id=1, source_target_pairs={{0,4},{1,5},{2,6},{3,7},{4,0},{5,1},{6,2},{7,3},{8,12},{9,13},{10,... | collective-permute-start | bytes 3145736 | tf_op jit(solution)/shard_map/ppermute | solution.py:489
  46.5 6.6 %collective-permute-start.5 = (f32[64,256]{1,0:T(8,128)S(1)}, f32[64,256]{1,0:T(8,128)S(1)}, u32[]{:S(2)}, u32[]{:S(2)}) collective-permute-start(f32[64,256]{1,0:T(8,128)S(1)} %get-tuple-element.81), channel_id=1, source_target_pairs={{0,1},{1,2},{2,3},{3,0},{4,5},{5,6},{6,7},{7,4},{8,9},{9,10},{10,1... | collective-permute-start | bytes 196616 | tf_op jit(solution)/shard_map/ppermute | solution.py:503
  48.1 16.4 %collective-permute-start.10 = (f32[128,384]{1,0:T(8,128)}, f32[128,384]{1,0:T(8,128)S(1)}, u32[]{:S(2)}, u32[]{:S(2)}) collective-permute-start(f32[128,384]{1,0:T(8,128)} %copy-done.30), channel_id=1, source_target_pairs={{0,2},{1,3},{2,0},{3,1},{4,6},{5,7},{6,4},{7,5},{8,10},{9,11},{10,... | collective-permute-start | bytes 589832 | tf_op jit(solution)/shard_map/ppermute | solution.py:503
  51.0 13.5 %collective-permute-start.11 = (f32[128,384]{1,0:T(8,128)}, f32[128,384]{1,0:T(8,128)S(1)}, u32[]{:S(2)}, u32[]{:S(2)}) collective-permute-start(f32[128,384]{1,0:T(8,128)} %copy-done.29), channel_id=1, source_target_pairs={{0,3},{1,0},{2,1},{3,2},{4,7},{5,4},{6,5},{7,6},{8,11},{9,8},{10,9... | collective-permute-start | bytes 589832 | tf_op jit(solution)/shard_map/ppermute | solution.py:503
  52.4 12.2 %collective-permute-start.9 = (f32[128,384]{1,0:T(8,128)}, f32[128,384]{1,0:T(8,128)S(1)}, u32[]{:S(2)}, u32[]{:S(2)}) collective-permute-start(f32[128,384]{1,0:T(8,128)} %copy-done.28), channel_id=1, source_target_pairs={{0,1},{1,2},{2,3},{3,0},{4,5},{5,6},{6,7},{7,4},{8,9},{9,10},{10,1... | collective-permute-start | bytes 589832 | tf_op jit(solution)/shard_map/ppermute | solution.py:503
  53.0 7.2 %collective-permute-start.6 = (f32[64,256]{1,0:T(8,128)S(1)}, f32[64,256]{1,0:T(8,128)S(1)}, u32[]{:S(2)}, u32[]{:S(2)}) collective-permute-start(f32[64,256]{1,0:T(8,128)S(1)} %get-tuple-element.82), channel_id=1, source_target_pairs={{0,2},{1,3},{2,0},{3,1},{4,6},{5,7},{6,4},{7,5},{8,10},{9,11},{10,... | collective-permute-start | bytes 196616 | tf_op jit(solution)/shard_map/ppermute | solution.py:503
  60.2 4.3 %collective-permute-start.7 = (f32[64,256]{1,0:T(8,128)S(1)}, f32[64,256]{1,0:T(8,128)S(1)}, u32[]{:S(2)}, u32[]{:S(2)}) collective-permute-start(f32[64,256]{1,0:T(8,128)S(1)} %get-tuple-element.83), channel_id=1, source_target_pairs={{0,3},{1,0},{2,1},{3,2},{4,7},{5,4},{6,5},{7,6},{8,11},{9,8},{10,9... | collective-permute-start | bytes 196616 | tf_op jit(solution)/shard_map/ppermute | solution.py:503
  69.8 29.0 %all-to-all-start.1 = ((f32[4,32,2048]{2,1,0:T(8,128)}), f32[4,32,2048]{2,1,0:T(8,128)S(1)}, u32[]{:S(2)}, u32[]{:S(2)}) async-start(f32[4,32,2048]{2,1,0:T(8,128)} %scan.1), calls=%async_computation.1 | async-start | bytes 2097152 | tf_op jit(solution)/shard_map/all_to_all | solution.py:531
  76.7 16.7 %collective-permute-start.15 = (f32[256,640]{1,0:T(8,128)}, f32[256,640]{1,0:T(8,128)S(1)}, u32[]{:S(2)}, u32[]{:S(2)}) collective-permute-start(f32[256,640]{1,0:T(8,128)} %copy-done.27), channel_id=1, source_target_pairs={{0,4},{1,5},{2,6},{3,7},{4,0},{5,1},{6,2},{7,3},{8,12},{9,13},{10,... | collective-permute-start | bytes 1966088 | tf_op jit(solution)/shard_map/ppermute | solution.py:489
  79.9 10.1 %collective-permute-start.12 = (f32[64,1024]{1,0:T(8,128)S(1)}, f32[64,1024]{1,0:T(8,128)S(1)}, u32[]{:S(2)}, u32[]{:S(2)}) collective-permute-start(f32[64,1024]{1,0:T(8,128)S(1)} %get-tuple-element.95), channel_id=1, source_target_pairs={{0,1},{1,2},{2,3},{3,0},{4,5},{5,6},{6,7},{7,4},{8,9},{9,10},{10,1... | collective-permute-start | bytes 786440 | tf_op jit(solution)/shard_map/ppermute | solution.py:503
  81.5 11.3 %collective-permute-start.13 = (f32[64,1024]{1,0:T(8,128)S(1)}, f32[64,1024]{1,0:T(8,128)S(1)}, u32[]{:S(2)}, u32[]{:S(2)}) collective-permute-start(f32[64,1024]{1,0:T(8,128)S(1)} %get-tuple-element.96), channel_id=1, source_target_pairs={{0,2},{1,3},{2,0},{3,1},{4,6},{5,7},{6,4},{7,5},{8,10},{9,11},{10,... | collective-permute-start | bytes 786440 | tf_op jit(solution)/shard_map/ppermute | solution.py:503
  84.4 8.4 %collective-permute-start.14 = (f32[64,1024]{1,0:T(8,128)S(1)}, f32[64,1024]{1,0:T(8,128)S(1)}, u32[]{:S(2)}, u32[]{:S(2)}) collective-permute-start(f32[64,1024]{1,0:T(8,128)S(1)} %get-tuple-element.97), channel_id=1, source_target_pairs={{0,3},{1,0},{2,1},{3,2},{4,7},{5,4},{6,5},{7,6},{8,11},{9,8},{10,9... | collective-permute-start | bytes 786440 | tf_op jit(solution)/shard_map/ppermute | solution.py:503
  85.8 7.1 %collective-permute-start.16 = (f32[64,384]{1,0:T(8,128)}, f32[64,384]{1,0:T(8,128)S(1)}, u32[]{:S(2)}, u32[]{:S(2)}) collective-permute-start(f32[64,384]{1,0:T(8,128)} %copy-done.31), channel_id=1, source_target_pairs={{0,4},{1,5},{2,6},{3,7},{4,0},{5,1},{6,2},{7,3},{8,12},{9,13},{10,... | collective-permute-start | bytes 294920 | tf_op jit(solution)/shard_map/ppermute | solution.py:489
  99.0 15.9 %collective-permute-start.17 = (f32[64,2048]{1,0:T(8,128)S(1)}, f32[64,2048]{1,0:T(8,128)S(1)}, u32[]{:S(2)}, u32[]{:S(2)}) collective-permute-start(f32[64,2048]{1,0:T(8,128)S(1)} %get-tuple-element.101), channel_id=1, source_target_pairs={{0,32},{32,64},{64,96},{96,128},{128,160},{160,192},{192,224},{224... | collective-permute-start | bytes 1572872 | tf_op jit(solution)/shard_map/ppermute | solution.py:538
  99.1 15.8 %collective-permute-start.18 = (f32[64,2048]{1,0:T(8,128)S(1)}, f32[64,2048]{1,0:T(8,128)S(1)}, u32[]{:S(2)}, u32[]{:S(2)}) collective-permute-start(f32[64,2048]{1,0:T(8,128)S(1)} %get-tuple-element.102), channel_id=1, source_target_pairs={{0,224},{32,0},{64,32},{96,64},{128,96},{160,128},{192,160},{224,1... | collective-permute-start | bytes 1572872 | tf_op jit(solution)/shard_map/ppermute | solution.py:539
  102.4 7.3 %collective-permute-start.19 = (f32[64,640]{1,0:T(8,128)S(1)}, f32[64,640]{1,0:T(8,128)S(1)}, u32[]{:S(2)}, u32[]{:S(2)}) collective-permute-start(f32[64,640]{1,0:T(8,128)S(1)} %get-tuple-element.110), channel_id=1, source_target_pairs={{0,1},{1,2},{2,3},{3,0},{4,5},{5,6},{6,7},{7,4},{8,9},{9,10},{10,1... | collective-permute-start | bytes 491528 | tf_op jit(solution)/shard_map/ppermute | solution.py:503
  104.0 9.9 %collective-permute-start.20 = (f32[64,640]{1,0:T(8,128)S(1)}, f32[64,640]{1,0:T(8,128)S(1)}, u32[]{:S(2)}, u32[]{:S(2)}) collective-permute-start(f32[64,640]{1,0:T(8,128)S(1)} %get-tuple-element.111), channel_id=1, source_target_pairs={{0,2},{1,3},{2,0},{3,1},{4,6},{5,7},{6,4},{7,5},{8,10},{9,11},{10,... | collective-permute-start | bytes 491528 | tf_op jit(solution)/shard_map/ppermute | solution.py:503
  106.9 7.0 %collective-permute-start.21 = (f32[64,640]{1,0:T(8,128)S(1)}, f32[64,640]{1,0:T(8,128)S(1)}, u32[]{:S(2)}, u32[]{:S(2)}) collective-permute-start(f32[64,640]{1,0:T(8,128)S(1)} %get-tuple-element.112), channel_id=1, source_target_pairs={{0,3},{1,0},{2,1},{3,2},{4,7},{5,4},{6,5},{7,6},{8,11},{9,8},{10,9... | collective-permute-start | bytes 491528 | tf_op jit(solution)/shard_map/ppermute | solution.py:503
  (32 other events, 219.1 us)

commit v2 on v1

--- a/solution.py
+++ b/solution.py
@@ -12,7 +12,7 @@
 RANK = 64
 ADAPTER_SCALE = 2.0
 EPS = 1e-06
-FIRST_BLOCK = 512
+FIRST_BLOCK = 256
 PART_COLUMNS = (256, 1024)
 SWAP_COLUMNS = 384
 VMEM_LIMIT = 16 * 1024 * 1024

time: 116 us -> 118 us (1.017)
  Pallas kernels: 13.6 us -> 15 us
    pallas_call x14, Pallas kernels: 13.6 us -> 15 us  [call(): pl.pallas_call(kernel, in_specs=[spec(i, far) for i in range(len(args))],...]
where the time goes in v2:
time: 118 us; the launch traced here: 117 us
  starting transfers between devices  49.6 us (42%)
  waiting for transfers between devices  37.2 us (32%)
  Pallas kernels  15 us (13%)
  local copies, waits for them, and re-layouts  13.7 us (12%)
    ppermute x12, starting transfers between devices, turned(): shares.append(lax.ppermute(value, 'dp', pairs))  22.4 us
    ppermute x12, waiting for transfers between devices, turned(): shares.append(lax.ppermute(value, 'dp', pairs))  18.6 us
    pallas_call x14, Pallas kernels, call(): pl.pallas_call(kernel, in_specs=[spec(i, far) for i in range(len(args))],...  15 us
    unnamed x64, local copies, waits for them, and re-layouts  13.7 us
    ppermute x4, waiting for transfers between devices, over(): return lax.ppermute(value, 'dp', pairs)  7.62 us
    all_to_all x1, starting transfers between devices, body(): lax.all_to_all(after, 'pipe', 0, 0, axis_index_groups=lines, tiled=True)  6.92 us
    all_to_all x1, starting transfers between devices, body(): lax.all_to_all(pair, 'pipe', 0, 0, axis_index_groups=lines, tiled=True)  5.48 us
    ppermute x1, waiting for transfers between devices, body(): there = lax.ppermute(here, 'tensor', far)  4.94 us
  transfers between devices with their start and end apart: 24, of which 11 were waited for; matrix products, arithmetic and copies ran while one was open for 0% of the time, Pallas kernels for 2%

profile of v2, /device:TPU:2, one launch (start us, length us, event | category | flops | bytes accessed | tf_op | source)
XLA Modules:
  0.0 117.4 jit_solution(9666280319585394708)
XLA Ops:
  0.6 8.4 %first.1 = (f32[256,2048]{1,0:T(8,128)}, bf16[256,2048]{1,0:T(8,128)(2,1)}, bf16[256,256]{1,0:T(8,128)(2,1)}, f32[256,512]{1,0:T(8,128)}, bf16[256,512]{1,0:T(8,128)(2,1)}, /*index=5*/f32[256,128]{1,0:T(8,128)}) custom-call(s32[4,4]{1,0:T(4,128)} %cand_hbm.1, s32[8]{0:T(128)} %counts_hbm.1, bf16[256,2048]{1,0:T(8,128)(2,1)} %bitcast.14, f32[1,2048]{1,0:T(1,128)} %gain_hbm.1, ...), custom_call_target="tpu_custom_call" | custom-call | tf_op jit(solution)/shard_map/first/pallas_call | solution.py:383
  9.2 1.5 %collective-permute-done = f32[256,128]{1,0:T(8,128)S(1)} collective-permute-done((f32[256,128]{1,0:T(8,128)}, f32[256,128]{1,0:T(8,128)S(1)}, u32[]{:S(2)}, u32[]{:S(2)}) %collective-permute-start) | collective-permute-done | bytes 131104 | tf_op jit(solution)/shard_map/ppermute | solution.py:456
  11.7 2.2 %collective-permute-start.1 = (f32[256,128]{1,0:T(8,128)S(1)}, f32[256,128]{1,0:T(8,128)S(1)}, u32[]{:S(2)}, u32[]{:S(2)}) collective-permute-start(f32[256,128]{1,0:T(8,128)S(1)} %add.3.here_ref), channel_id=1, source_target_pairs={{0,16},{8,24},{16,0},{24,8},{1,17},{9,25},{17,1},{25,9},{2,18},{10... | collective-permute-start | bytes 393224 | tf_op jit(solution)/shard_map/ppermute | solution.py:457
  13.9 4.9 %collective-permute-done.1.there_ref = f32[256,128]{1,0:T(8,128)S(1)} collective-permute-done((f32[256,128]{1,0:T(8,128)S(1)}, f32[256,128]{1,0:T(8,128)S(1)}, u32[]{:S(2)}, u32[]{:S(2)}) %collective-permute-start.1) | collective-permute-done | bytes 131104 | tf_op jit(solution)/shard_map/ppermute | solution.py:457
  18.8 1.6 %copy-done.1 = f32[256,2048]{1,0:T(8,128)S(1)} copy-done((f32[256,2048]{1,0:T(8,128)S(1)}, f32[256,2048]{1,0:T(8,128)}, u32[]{:S(2)}) %copy-start.1) | copy-done | bytes 2097176
  21.2 2.0 %collective-permute-start.2 = (f32[64,2048]{1,0:T(8,128)S(1)}, f32[64,2048]{1,0:T(8,128)S(1)}, u32[]{:S(2)}, u32[]{:S(2)}) collective-permute-start(f32[64,2048]{1,0:T(8,128)S(1)} %get-tuple-element.63.up_ref), channel_id=1, source_target_pairs={{0,32},{32,64},{64,96},{96,128},{128,160},{160,192},{192,224},{224... | collective-permute-start | bytes 1572872 | tf_op jit(solution)/shard_map/ppermute | solution.py:470
  23.2 4.0 %collective-permute-start.3 = (f32[64,2048]{1,0:T(8,128)S(1)}, f32[64,2048]{1,0:T(8,128)S(1)}, u32[]{:S(2)}, u32[]{:S(2)}) collective-permute-start(f32[64,2048]{1,0:T(8,128)S(1)} %get-tuple-element.64.down_ref), channel_id=1, source_target_pairs={{0,224},{32,0},{64,32},{96,64},{128,96},{160,128},{192,160},{224,1... | collective-permute-start | bytes 1572872 | tf_op jit(solution)/shard_map/ppermute | solution.py:471
  32.3 6.7 %collective-permute-done.4.come_ref = f32[256,256]{1,0:T(8,128)S(1)} collective-permute-done((f32[256,256]{1,0:T(8,128)S(1)}, f32[256,256]{1,0:T(8,128)S(1)}, u32[]{:S(2)}, u32[]{:S(2)}) %collective-permute-start.4) | collective-permute-done | bytes 262176 | tf_op jit(solution)/shard_map/ppermute | solution.py:489
  40.9 5.5 %all-to-all-start = ((f32[4,32,2048]{2,1,0:T(8,128)}), f32[4,32,2048]{2,1,0:T(8,128)S(1)}, u32[]{:S(2)}, u32[]{:S(2)}) async-start(f32[4,32,2048]{2,1,0:T(8,128)} %pair.1), calls=%async_computation | async-start | bytes 2097152 | tf_op jit(solution)/shard_map/all_to_all | solution.py:517
  47.9 1.7 %collective-permute-start.5 = (f32[64,256]{1,0:T(8,128)S(1)}, f32[64,256]{1,0:T(8,128)S(1)}, u32[]{:S(2)}, u32[]{:S(2)}) collective-permute-start(f32[64,256]{1,0:T(8,128)S(1)} %get-tuple-element.81), channel_id=1, source_target_pairs={{0,1},{1,2},{2,3},{3,0},{4,5},{5,6},{6,7},{7,4},{8,9},{9,10},{10,1... | collective-permute-start | bytes 196616 | tf_op jit(solution)/shard_map/ppermute | solution.py:503
  49.5 2.9 %collective-permute-start.10 = (f32[128,384]{1,0:T(8,128)}, f32[128,384]{1,0:T(8,128)S(1)}, u32[]{:S(2)}, u32[]{:S(2)}) collective-permute-start(f32[128,384]{1,0:T(8,128)} %copy-done.30), channel_id=1, source_target_pairs={{0,2},{1,3},{2,0},{3,1},{4,6},{5,7},{6,4},{7,5},{8,10},{9,11},{10,... | collective-permute-start | bytes 589832 | tf_op jit(solution)/shard_map/ppermute | solution.py:503
  54.5 2.9 %collective-permute-start.6 = (f32[64,256]{1,0:T(8,128)S(1)}, f32[64,256]{1,0:T(8,128)S(1)}, u32[]{:S(2)}, u32[]{:S(2)}) collective-permute-start(f32[64,256]{1,0:T(8,128)S(1)} %get-tuple-element.82), channel_id=1, source_target_pairs={{0,2},{1,3},{2,0},{3,1},{4,6},{5,7},{6,4},{7,5},{8,10},{9,11},{10,... | collective-permute-start | bytes 196616 | tf_op jit(solution)/shard_map/ppermute | solution.py:503
  57.3 4.3 %collective-permute-done.6.refs_2_ = f32[64,256]{1,0:T(8,128)S(1)} collective-permute-done((f32[64,256]{1,0:T(8,128)S(1)}, f32[64,256]{1,0:T(8,128)S(1)}, u32[]{:S(2)}, u32[]{:S(2)}) %collective-permute-start.6) | collective-permute-done | bytes 65568 | tf_op jit(solution)/shard_map/ppermute | solution.py:503
  62.8 3.1 %collective-permute-done.7.refs_3_ = f32[64,256]{1,0:T(8,128)S(1)} collective-permute-done((f32[64,256]{1,0:T(8,128)S(1)}, f32[64,256]{1,0:T(8,128)S(1)}, u32[]{:S(2)}, u32[]{:S(2)}) %collective-permute-start.7) | collective-permute-done | bytes 65568 | tf_op jit(solution)/shard_map/ppermute | solution.py:503
  71.2 6.9 %all-to-all-start.1 = ((f32[4,32,2048]{2,1,0:T(8,128)}), f32[4,32,2048]{2,1,0:T(8,128)S(1)}, u32[]{:S(2)}, u32[]{:S(2)}) async-start(f32[4,32,2048]{2,1,0:T(8,128)} %scan.1), calls=%async_computation.1 | async-start | bytes 2097152 | tf_op jit(solution)/shard_map/all_to_all | solution.py:531
  81.3 1.6 %collective-permute-start.12 = (f32[64,1024]{1,0:T(8,128)S(1)}, f32[64,1024]{1,0:T(8,128)S(1)}, u32[]{:S(2)}, u32[]{:S(2)}) collective-permute-start(f32[64,1024]{1,0:T(8,128)S(1)} %get-tuple-element.95), channel_id=1, source_target_pairs={{0,1},{1,2},{2,3},{3,0},{4,5},{5,6},{6,7},{7,4},{8,9},{9,10},{10,1... | collective-permute-start | bytes 786440 | tf_op jit(solution)/shard_map/ppermute | solution.py:503
  82.9 2.9 %collective-permute-start.13 = (f32[64,1024]{1,0:T(8,128)S(1)}, f32[64,1024]{1,0:T(8,128)S(1)}, u32[]{:S(2)}, u32[]{:S(2)}) collective-permute-start(f32[64,1024]{1,0:T(8,128)S(1)} %get-tuple-element.96), channel_id=1, source_target_pairs={{0,2},{1,3},{2,0},{3,1},{4,6},{5,7},{6,4},{7,5},{8,10},{9,11},{10,... | collective-permute-start | bytes 786440 | tf_op jit(solution)/shard_map/ppermute | solution.py:503
  88.7 2.7 %collective-permute-done.12.refs_1_ = f32[64,1024]{1,0:T(8,128)S(1)} collective-permute-done((f32[64,1024]{1,0:T(8,128)S(1)}, f32[64,1024]{1,0:T(8,128)S(1)}, u32[]{:S(2)}, u32[]{:S(2)}) %collective-permute-start.12) | collective-permute-done | bytes 262176 | tf_op jit(solution)/shard_map/ppermute | solution.py:503
  91.4 2.8 %collective-permute-done.13.refs_2_ = f32[64,1024]{1,0:T(8,128)S(1)} collective-permute-done((f32[64,1024]{1,0:T(8,128)S(1)}, f32[64,1024]{1,0:T(8,128)S(1)}, u32[]{:S(2)}, u32[]{:S(2)}) %collective-permute-start.13) | collective-permute-done | bytes 262176 | tf_op jit(solution)/shard_map/ppermute | solution.py:503
  95.8 4.4 %all-to-all-done.1.after_ref = f32[4,32,2048]{2,1,0:T(8,128)S(1)} async-done(((f32[4,32,2048]{2,1,0:T(8,128)}), f32[4,32,2048]{2,1,0:T(8,128)S(1)}, u32[]{:S(2)}, u32[]{:S(2)}) %all-to-all-start.1) | async-done | bytes 1048608 | tf_op jit(solution)/shard_map/all_to_all | solution.py:531
  100.5 3.2 %collective-permute-start.18 = (f32[64,2048]{1,0:T(8,128)S(1)}, f32[64,2048]{1,0:T(8,128)S(1)}, u32[]{:S(2)}, u32[]{:S(2)}) collective-permute-start(f32[64,2048]{1,0:T(8,128)S(1)} %get-tuple-element.102), channel_id=1, source_target_pairs={{0,224},{32,0},{64,32},{96,64},{128,96},{160,128},{192,160},{224,1... | collective-permute-start | bytes 1572872 | tf_op jit(solution)/shard_map/ppermute | solution.py:539
  103.8 1.7 %collective-permute-start.19 = (f32[64,640]{1,0:T(8,128)S(1)}, f32[64,640]{1,0:T(8,128)S(1)}, u32[]{:S(2)}, u32[]{:S(2)}) collective-permute-start(f32[64,640]{1,0:T(8,128)S(1)} %get-tuple-element.110), channel_id=1, source_target_pairs={{0,1},{1,2},{2,3},{3,0},{4,5},{5,6},{6,7},{7,4},{8,9},{9,10},{10,1... | collective-permute-start | bytes 491528 | tf_op jit(solution)/shard_map/ppermute | solution.py:503
  105.4 2.9 %collective-permute-start.20 = (f32[64,640]{1,0:T(8,128)S(1)}, f32[64,640]{1,0:T(8,128)S(1)}, u32[]{:S(2)}, u32[]{:S(2)}) collective-permute-start(f32[64,640]{1,0:T(8,128)S(1)} %get-tuple-element.111), channel_id=1, source_target_pairs={{0,2},{1,3},{2,0},{3,1},{4,6},{5,7},{6,4},{7,5},{8,10},{9,11},{10,... | collective-permute-start | bytes 491528 | tf_op jit(solution)/shard_map/ppermute | solution.py:503
  111.1 4.2 %collective-permute-done.20.refs_2_ = f32[64,640]{1,0:T(8,128)S(1)} collective-permute-done((f32[64,640]{1,0:T(8,128)S(1)}, f32[64,640]{1,0:T(8,128)S(1)}, u32[]{:S(2)}, u32[]{:S(2)}) %collective-permute-start.20) | collective-permute-done | bytes 163872 | tf_op jit(solution)/shard_map/ppermute | solution.py:503
  (103 shorter events, 31.3 us)
Async XLA Ops:
  9.1 1.6 %collective-permute-start = (f32[256,128]{1,0:T(8,128)}, f32[256,128]{1,0:T(8,128)S(1)}, u32[]{:S(2)}, u32[]{:S(2)}) collective-permute-start(f32[256,128]{1,0:T(8,128)} %get-tuple-element.59), channel_id=1, source_target_pairs={{0,8},{8,0},{16,24},{24,16},{1,9},{9,1},{17,25},{25,17},{2,10},{10... | collective-permute-start | bytes 393224 | tf_op jit(solution)/shard_map/ppermute | solution.py:456
  11.7 7.1 %collective-permute-start.1 = (f32[256,128]{1,0:T(8,128)S(1)}, f32[256,128]{1,0:T(8,128)S(1)}, u32[]{:S(2)}, u32[]{:S(2)}) collective-permute-start(f32[256,128]{1,0:T(8,128)S(1)} %add.3.here_ref), channel_id=1, source_target_pairs={{0,16},{8,24},{16,0},{24,8},{1,17},{9,25},{17,1},{25,9},{2,18},{10... | collective-permute-start | bytes 393224 | tf_op jit(solution)/shard_map/ppermute | solution.py:457
  21.2 18.5 %collective-permute-start.2 = (f32[64,2048]{1,0:T(8,128)S(1)}, f32[64,2048]{1,0:T(8,128)S(1)}, u32[]{:S(2)}, u32[]{:S(2)}) collective-permute-start(f32[64,2048]{1,0:T(8,128)S(1)} %get-tuple-element.63.up_ref), channel_id=1, source_target_pairs={{0,32},{32,64},{64,96},{96,128},{128,160},{160,192},{192,224},{224... | collective-permute-start | bytes 1572872 | tf_op jit(solution)/shard_map/ppermute | solution.py:470
  23.2 16.5 %collective-permute-start.3 = (f32[64,2048]{1,0:T(8,128)S(1)}, f32[64,2048]{1,0:T(8,128)S(1)}, u32[]{:S(2)}, u32[]{:S(2)}) collective-permute-start(f32[64,2048]{1,0:T(8,128)S(1)} %get-tuple-element.64.down_ref), channel_id=1, source_target_pairs={{0,224},{32,0},{64,32},{96,64},{128,96},{160,128},{192,160},{224,1... | collective-permute-start | bytes 1572872 | tf_op jit(solution)/shard_map/ppermute | solution.py:471
  31.7 7.3 %collective-permute-start.4 = (f32[256,256]{1,0:T(8,128)S(1)}, f32[256,256]{1,0:T(8,128)S(1)}, u32[]{:S(2)}, u32[]{:S(2)}) collective-permute-start(f32[256,256]{1,0:T(8,128)S(1)} %get-tuple-element.69), channel_id=1, source_target_pairs={{0,4},{1,5},{2,6},{3,7},{4,0},{5,1},{6,2},{7,3},{8,12},{9,13},{10,... | collective-permute-start | bytes 786440 | tf_op jit(solution)/shard_map/ppermute | solution.py:489
  40.9 29.3 %all-to-all-start = ((f32[4,32,2048]{2,1,0:T(8,128)}), f32[4,32,2048]{2,1,0:T(8,128)S(1)}, u32[]{:S(2)}, u32[]{:S(2)}) async-start(f32[4,32,2048]{2,1,0:T(8,128)} %pair.1), calls=%async_computation | async-start | bytes 2097152 | tf_op jit(solution)/shard_map/all_to_all | solution.py:517
  46.3 22.8 %collective-permute-start.8 = (f32[256,1024]{1,0:T(8,128)}, f32[256,1024]{1,0:T(8,128)S(1)}, u32[]{:S(2)}, u32[]{:S(2)}) collective-permute-start(f32[256,1024]{1,0:T(8,128)} %copy-done.26), channel_id=1, source_target_pairs={{0,4},{1,5},{2,6},{3,7},{4,0},{5,1},{6,2},{7,3},{8,12},{9,13},{10,... | collective-permute-start | bytes 3145736 | tf_op jit(solution)/shard_map/ppermute | solution.py:489
  47.9 6.6 %collective-permute-start.5 = (f32[64,256]{1,0:T(8,128)S(1)}, f32[64,256]{1,0:T(8,128)S(1)}, u32[]{:S(2)}, u32[]{:S(2)}) collective-permute-start(f32[64,256]{1,0:T(8,128)S(1)} %get-tuple-element.81), channel_id=1, source_target_pairs={{0,1},{1,2},{2,3},{3,0},{4,5},{5,6},{6,7},{7,4},{8,9},{9,10},{10,1... | collective-permute-start | bytes 196616 | tf_op jit(solution)/shard_map/ppermute | solution.py:503
  49.5 16.4 %collective-permute-start.10 = (f32[128,384]{1,0:T(8,128)}, f32[128,384]{1,0:T(8,128)S(1)}, u32[]{:S(2)}, u32[]{:S(2)}) collective-permute-start(f32[128,384]{1,0:T(8,128)} %copy-done.30), channel_id=1, source_target_pairs={{0,2},{1,3},{2,0},{3,1},{4,6},{5,7},{6,4},{7,5},{8,10},{9,11},{10,... | collective-permute-start | bytes 589832 | tf_op jit(solution)/shard_map/ppermute | solution.py:503
  52.4 13.5 %collective-permute-start.11 = (f32[128,384]{1,0:T(8,128)}, f32[128,384]{1,0:T(8,128)S(1)}, u32[]{:S(2)}, u32[]{:S(2)}) collective-permute-start(f32[128,384]{1,0:T(8,128)} %copy-done.29), channel_id=1, source_target_pairs={{0,3},{1,0},{2,1},{3,2},{4,7},{5,4},{6,5},{7,6},{8,11},{9,8},{10,9... | collective-permute-start | bytes 589832 | tf_op jit(solution)/shard_map/ppermute | solution.py:503
  53.8 12.2 %collective-permute-start.9 = (f32[128,384]{1,0:T(8,128)}, f32[128,384]{1,0:T(8,128)S(1)}, u32[]{:S(2)}, u32[]{:S(2)}) collective-permute-start(f32[128,384]{1,0:T(8,128)} %copy-done.28), channel_id=1, source_target_pairs={{0,1},{1,2},{2,3},{3,0},{4,5},{5,6},{6,7},{7,4},{8,9},{9,10},{10,1... | collective-permute-start | bytes 589832 | tf_op jit(solution)/shard_map/ppermute | solution.py:503
  54.5 7.2 %collective-permute-start.6 = (f32[64,256]{1,0:T(8,128)S(1)}, f32[64,256]{1,0:T(8,128)S(1)}, u32[]{:S(2)}, u32[]{:S(2)}) collective-permute-start(f32[64,256]{1,0:T(8,128)S(1)} %get-tuple-element.82), channel_id=1, source_target_pairs={{0,2},{1,3},{2,0},{3,1},{4,6},{5,7},{6,4},{7,5},{8,10},{9,11},{10,... | collective-permute-start | bytes 196616 | tf_op jit(solution)/shard_map/ppermute | solution.py:503
  61.7 4.3 %collective-permute-start.7 = (f32[64,256]{1,0:T(8,128)S(1)}, f32[64,256]{1,0:T(8,128)S(1)}, u32[]{:S(2)}, u32[]{:S(2)}) collective-permute-start(f32[64,256]{1,0:T(8,128)S(1)} %get-tuple-element.83), channel_id=1, source_target_pairs={{0,3},{1,0},{2,1},{3,2},{4,7},{5,4},{6,5},{7,6},{8,11},{9,8},{10,9... | collective-permute-start | bytes 196616 | tf_op jit(solution)/shard_map/ppermute | solution.py:503
  71.2 29.0 %all-to-all-start.1 = ((f32[4,32,2048]{2,1,0:T(8,128)}), f32[4,32,2048]{2,1,0:T(8,128)S(1)}, u32[]{:S(2)}, u32[]{:S(2)}) async-start(f32[4,32,2048]{2,1,0:T(8,128)} %scan.1), calls=%async_computation.1 | async-start | bytes 2097152 | tf_op jit(solution)/shard_map/all_to_all | solution.py:531
  78.2 16.7 %collective-permute-start.15 = (f32[256,640]{1,0:T(8,128)}, f32[256,640]{1,0:T(8,128)S(1)}, u32[]{:S(2)}, u32[]{:S(2)}) collective-permute-start(f32[256,640]{1,0:T(8,128)} %copy-done.27), channel_id=1, source_target_pairs={{0,4},{1,5},{2,6},{3,7},{4,0},{5,1},{6,2},{7,3},{8,12},{9,13},{10,... | collective-permute-start | bytes 1966088 | tf_op jit(solution)/shard_map/ppermute | solution.py:489
  81.3 10.1 %collective-permute-start.12 = (f32[64,1024]{1,0:T(8,128)S(1)}, f32[64,1024]{1,0:T(8,128)S(1)}, u32[]{:S(2)}, u32[]{:S(2)}) collective-permute-start(f32[64,1024]{1,0:T(8,128)S(1)} %get-tuple-element.95), channel_id=1, source_target_pairs={{0,1},{1,2},{2,3},{3,0},{4,5},{5,6},{6,7},{7,4},{8,9},{9,10},{10,1... | collective-permute-start | bytes 786440 | tf_op jit(solution)/shard_map/ppermute | solution.py:503
  82.9 11.2 %collective-permute-start.13 = (f32[64,1024]{1,0:T(8,128)S(1)}, f32[64,1024]{1,0:T(8,128)S(1)}, u32[]{:S(2)}, u32[]{:S(2)}) collective-permute-start(f32[64,1024]{1,0:T(8,128)S(1)} %get-tuple-element.96), channel_id=1, source_target_pairs={{0,2},{1,3},{2,0},{3,1},{4,6},{5,7},{6,4},{7,5},{8,10},{9,11},{10,... | collective-permute-start | bytes 786440 | tf_op jit(solution)/shard_map/ppermute | solution.py:503
  85.8 8.3 %collective-permute-start.14 = (f32[64,1024]{1,0:T(8,128)S(1)}, f32[64,1024]{1,0:T(8,128)S(1)}, u32[]{:S(2)}, u32[]{:S(2)}) collective-permute-start(f32[64,1024]{1,0:T(8,128)S(1)} %get-tuple-element.97), channel_id=1, source_target_pairs={{0,3},{1,0},{2,1},{3,2},{4,7},{5,4},{6,5},{7,6},{8,11},{9,8},{10,9... | collective-permute-start | bytes 786440 | tf_op jit(solution)/shard_map/ppermute | solution.py:503
  87.2 7.0 %collective-permute-start.16 = (f32[64,384]{1,0:T(8,128)}, f32[64,384]{1,0:T(8,128)S(1)}, u32[]{:S(2)}, u32[]{:S(2)}) collective-permute-start(f32[64,384]{1,0:T(8,128)} %copy-done.31), channel_id=1, source_target_pairs={{0,4},{1,5},{2,6},{3,7},{4,0},{5,1},{6,2},{7,3},{8,12},{9,13},{10,... | collective-permute-start | bytes 294920 | tf_op jit(solution)/shard_map/ppermute | solution.py:489
  100.4 15.8 %collective-permute-start.17 = (f32[64,2048]{1,0:T(8,128)S(1)}, f32[64,2048]{1,0:T(8,128)S(1)}, u32[]{:S(2)}, u32[]{:S(2)}) collective-permute-start(f32[64,2048]{1,0:T(8,128)S(1)} %get-tuple-element.101), channel_id=1, source_target_pairs={{0,32},{32,64},{64,96},{96,128},{128,160},{160,192},{192,224},{224... | collective-permute-start | bytes 1572872 | tf_op jit(solution)/shard_map/ppermute | solution.py:538
  100.5 15.8 %collective-permute-start.18 = (f32[64,2048]{1,0:T(8,128)S(1)}, f32[64,2048]{1,0:T(8,128)S(1)}, u32[]{:S(2)}, u32[]{:S(2)}) collective-permute-start(f32[64,2048]{1,0:T(8,128)S(1)} %get-tuple-element.102), channel_id=1, source_target_pairs={{0,224},{32,0},{64,32},{96,64},{128,96},{160,128},{192,160},{224,1... | collective-permute-start | bytes 1572872 | tf_op jit(solution)/shard_map/ppermute | solution.py:539
  103.8 7.3 %collective-permute-start.19 = (f32[64,640]{1,0:T(8,128)S(1)}, f32[64,640]{1,0:T(8,128)S(1)}, u32[]{:S(2)}, u32[]{:S(2)}) collective-permute-start(f32[64,640]{1,0:T(8,128)S(1)} %get-tuple-element.110), channel_id=1, source_target_pairs={{0,1},{1,2},{2,3},{3,0},{4,5},{5,6},{6,7},{7,4},{8,9},{9,10},{10,1... | collective-permute-start | bytes 491528 | tf_op jit(solution)/shard_map/ppermute | solution.py:503
  105.4 9.9 %collective-permute-start.20 = (f32[64,640]{1,0:T(8,128)S(1)}, f32[64,640]{1,0:T(8,128)S(1)}, u32[]{:S(2)}, u32[]{:S(2)}) collective-permute-start(f32[64,640]{1,0:T(8,128)S(1)} %get-tuple-element.111), channel_id=1, source_target_pairs={{0,2},{1,3},{2,0},{3,1},{4,6},{5,7},{6,4},{7,5},{8,10},{9,11},{10,... | collective-permute-start | bytes 491528 | tf_op jit(solution)/shard_map/ppermute | solution.py:503
  108.3 7.0 %collective-permute-start.21 = (f32[64,640]{1,0:T(8,128)S(1)}, f32[64,640]{1,0:T(8,128)S(1)}, u32[]{:S(2)}, u32[]{:S(2)}) collective-permute-start(f32[64,640]{1,0:T(8,128)S(1)} %get-tuple-element.112), channel_id=1, source_target_pairs={{0,3},{1,0},{2,1},{3,2},{4,7},{5,4},{6,5},{7,6},{8,11},{9,8},{10,9... | collective-permute-start | bytes 491528 | tf_op jit(solution)/shard_map/ppermute | solution.py:503
  (32 other events, 220.4 us)
